TPU v7x, 32 devices: a whole 2x2x4 slice. The times are simulated.
32 devices in a mesh: groups: 2 (over x), chan: 16 (over z, y, core).
Axes of the slice: x: 2, y: 2, z: 4, core: 2. Of those that a mesh axis runs over, the one named last changes fastest.
Arguments:
- snapshots: bfloat16 [4, 4096, 4096], P('groups', 'chan'), parts along dimension 0, may hold values from -6 to 6
- freq_bins: int32 [512], replicated, may hold values from 1 to 2047
- mode_shapes: bfloat16 [8, 64, 4096], P(None, None, 'chan'), may hold values from -8 to 8
- mode_counts: int32 [8], replicated, may hold values from 16 to 64
- wavenumbers: float32 [8, 64, 512], replicated, may hold values from 20 to 200
- source_modes: float32 [8, 64, 128], replicated, may hold values from -5 to 5
- segment_owner: int32 [4], replicated, may hold values from 0 to 7
Outputs:
- localization: float32 [32, 128], P(('groups', 'chan')), parts along dimension 0
There are 2 independent parts, one for each index of `groups`. A program takes and returns all parts, laid end to end along the dimension named above; an argument that names none is the same for every part. Nothing has to cross between parts.
All inputs are finite; a program needn't handle non-finite values.
Results may differ from a plain program's by a relative error of at most 0.0019.
Values may be sent and summed in bfloat16 or wider, within the bound.
A program may use at most 128 MiB of HBM per device.

v0:
```python
import jax
import jax.numpy as jnp
from jax import lax
from jax.sharding import PartitionSpec as P

F = 512
RPB = 4


range_start = 1.0
range_step = 0.01


def dft_table(freq_bins, samples):
    sample_ids = jnp.arange(samples, dtype=jnp.int32)
    residue = freq_bins[:, None] * sample_ids[None, :] % samples
    angles = residue.astype(jnp.float32) * (2.0 * jnp.pi / samples)
    return jnp.stack([jnp.cos(angles), -jnp.sin(angles)]).astype(jnp.bfloat16)


def surface_terms(
    proj_flat,
    gram_rounded,
    traces,
    waves,
    source_modes,
    mode_counts,
    segment_owner,
    ranges_per_block,
    freq_total,
):
    segs, modes, depths = source_modes.shape
    freqs = proj_flat.shape[0]
    snaps = proj_flat.shape[2]
    highest = lax.Precision.HIGHEST
    proj_four = proj_flat.reshape(freqs, 2, snaps, segs, modes)
    proj_real = proj_four[:, 0]
    proj_imag = proj_four[:, 1]
    upper = jnp.concatenate([proj_real, proj_imag], axis=-1)
    lower = jnp.concatenate([proj_imag, -proj_real], axis=-1)
    coupling = jnp.concatenate([upper, lower], axis=1)
    coupling = jnp.transpose(coupling, (2, 0, 1, 3)).astype(jnp.float32)
    zero_block = jnp.zeros_like(gram_rounded)
    gram_double = jnp.concatenate(
        [
            jnp.concatenate([gram_rounded, zero_block], axis=2),
            jnp.concatenate([zero_block, gram_rounded], axis=2),
        ],
        axis=1,
    ).astype(jnp.float32)
    active = (jnp.arange(modes, dtype=jnp.int32)[None, :] < mode_counts[:, None]).astype(
        jnp.float32
    )
    masked = jnp.transpose(source_modes * active[:, :, None], (0, 2, 1))
    mode_double = jnp.concatenate([masked, masked], axis=-1)
    wave_t = jnp.transpose(waves, (0, 2, 1))
    wave_double = jnp.concatenate([wave_t, wave_t], axis=-1)
    lanes = jnp.arange(2 * modes, dtype=jnp.int32) < modes
    seg_ids = jnp.arange(segs, dtype=jnp.int32)
    blocks = segment_owner.shape[0]

    def one_block(items):
        block_id, owner = items
        pick = (seg_ids == owner).astype(jnp.float32)
        wave_block = jnp.einsum("s,sfm->fm", pick, wave_double, precision=highest)
        mode_block = jnp.einsum("s,szm->zm", pick, mode_double, precision=highest)
        coupling_block = jnp.einsum("s,sfkm->fkm", pick, coupling, precision=highest).astype(
            jnp.bfloat16
        )
        gram_block = jnp.einsum("s,smn->mn", pick, gram_double, precision=highest).astype(
            jnp.bfloat16
        )
        range_ids = block_id * ranges_per_block + jnp.arange(ranges_per_block, dtype=jnp.int32)
        ranges = range_start + range_step * range_ids.astype(jnp.float32)
        phases = wave_block[:, None, :] * ranges[None, :, None]
        trig = jnp.where(lanes[None, None, :], jnp.cos(phases), jnp.sin(phases))
        amplitude = mode_block[None, None, :, :] / jnp.sqrt(phases)[:, :, None, :]
        cells = ranges_per_block * depths
        replica = (
            (amplitude * trig[:, :, None, :]).reshape(freqs, cells, 2 * modes).astype(jnp.bfloat16)
        )
        beams = jnp.einsum(
            "fkm,fcm->fkc", coupling_block, replica, preferred_element_type=jnp.float32
        )
        powers = jnp.sum(beams * beams, axis=1)
        mapped = jnp.einsum("fcm,mn->fcn", replica, gram_block, preferred_element_type=jnp.float32)
        weight_norm = jnp.sum(replica.astype(jnp.float32) * mapped, axis=-1)
        bartlett = powers / (snaps * traces[:, None] * weight_norm)
        return (jnp.sum(bartlett, axis=0) / freq_total).reshape(ranges_per_block, depths)

    block_ids = jnp.arange(blocks, dtype=jnp.int32)
    parts = lax.map(one_block, (block_ids, segment_owner))
    return parts.reshape(blocks * ranges_per_block, depths)


def per_device(
    snapshots, freq_bins, mode_shapes, mode_counts, wavenumbers, source_modes, segment_owner
):
    devices_chan = lax.axis_size("chan")
    samples = snapshots.shape[2]
    segs = mode_shapes.shape[0]
    modes = mode_shapes.shape[1]
    local_freqs = F // devices_chan
    table_values = dft_table(freq_bins, samples)
    spectra = jnp.einsum(
        "cft,lht->cflh", table_values, snapshots, preferred_element_type=jnp.float32
    ).astype(jnp.bfloat16)
    moved = lax.all_to_all(spectra, "chan", split_axis=1, concat_axis=3, tiled=True)
    traces = jnp.sum(jnp.square(moved.astype(jnp.float32)), axis=(0, 2, 3))
    piece = lax.all_gather(mode_shapes, "chan", axis=2, tiled=True)
    flat_piece = piece.reshape(segs * modes, piece.shape[2])
    projections = jnp.einsum("cflh,kh->fclk", moved, flat_piece, preferred_element_type=jnp.float32)
    proj_rounded = projections.astype(jnp.bfloat16)
    local_gram = jnp.einsum(
        "smh,snh->smn", mode_shapes, mode_shapes, preferred_element_type=jnp.float32
    )
    gram = lax.psum(local_gram.reshape(segs, modes * modes), "chan")
    gram_rounded = gram.reshape(segs, modes, modes).astype(jnp.bfloat16)
    first_freq = lax.axis_index("chan") * local_freqs
    local_waves = lax.dynamic_slice_in_dim(wavenumbers, first_freq, local_freqs, 2)
    partial_surface = surface_terms(
        proj_rounded,
        gram_rounded,
        traces,
        local_waves,
        source_modes,
        mode_counts,
        segment_owner,
        RPB,
        F,
    )
    own_rows = partial_surface.shape[0] // devices_chan
    total_surface = lax.psum(partial_surface, "chan")
    highest_value = jnp.max(total_surface)
    own_surface = lax.dynamic_slice_in_dim(
        total_surface, lax.axis_index("chan") * own_rows, own_rows, 0
    )
    return own_surface / highest_value


def solution(mesh):
    return jax.shard_map(
        per_device,
        mesh=mesh,
        in_specs=(P("groups", "chan", None), P(), P(None, None, "chan"), P(), P(), P(), P()),
        out_specs=P(("groups", "chan"), None),
        check_vma=False,
    )
```

profile of v0, /device:TPU:0, one launch (start us, length us, event | category | flops | bytes accessed | tf_op | source)
XLA Modules:
  0.0 447.2 jit_solution(17609144802344206183)
XLA Ops:
  7.3 35.6 %cosine_convert_fusion = (bf16[1,512,4096]{2,1,0:T(8,128)(2,1)S(1)}, bf16[1,512,4096]{2,1,0:T(8,128)(2,1)S(1)}) fusion(s32[512]{0:T(512)} %param.10), kind=kLoop, calls=%fused_computation.48 | loop fusion | flops 35651584 | bytes 8390656 | tf_op jit(solution)/shard_map/convert.1
  42.9 4.5 %fusion.36 = bf16[2,512,2,256]{3,1,2,0:T(8,128)(2,1)S(1)} fusion(bf16[2,256,4096]{2,1,0:T(8,128)(2,1)S(1)} %copy-done.8, bf16[1,512,4096]{2,1,0:T(8,128)(2,1)S(1)} %get-tuple-element.107, bf16[1,512,4096]{2,1,0:T(8,128)(2,1)S(1)} %get-tuple-element.106), kind=kOutput, calls=%fused_computation.54 | convolution fusion | flops 4312268800 | bytes 13631488 | tf_op jit(solution)/shard_map/cft,lht->cflh/dot_general | solution.py:105
  47.4 2.1 copy.25
  49.5 7.4 %all-to-all-start = ((bf16[2,512,2,256]{3,2,0,1:T(2,128)(2,1)}), bf16[2,512,2,256]{3,2,0,1:T(2,128)(2,1)S(1)}, u32[]{:S(2)}, u32[]{:S(2)}) async-start(bf16[2,512,2,256]{3,2,0,1:T(2,128)(2,1)} %copy.25), calls=%async_computation | async-start | bytes 2097152 | tf_op jit(solution)/shard_map/all_to_all | solution.py:108
  57.7 75.9 %all-reduce.3 = bf16[8,4096]{1,0:T(8,128)(2,1)S(1)} all-reduce(f32[8,4096]{1,0:T(8,128)S(1)} %reshape.173), channel_id=1, replica_groups=mesh['groups'=2,'chan'=16] {'chan'}, use_global_device_ids=true, to_apply=%region_0.1 | all-reduce | flops 32768 | bytes 196608 | tf_op jit(solution)/shard_map/psum | solution.py:117
  137.9 4.0 fusion.39
  142.6 1.7 convert_bitcast_fusion
  144.3 264.0 %while.11 = (s32[]{:T(128)}, f32[4,4,128]{2,1,0:T(4,128)S(1)}, s32[4]{0:T(128)S(1)}, f32[8,32,4,128]{3,2,1,0:T(4,128)}, f32[8,128,128]{2,1,0:T(8,128)S(1)}, /*in...) while((s32[]{:T(128)}, f32[4,4,128]{2,1,0:T(4,128)S(1)}, ...), condition=%wide.region_6.7_spmd.clone, body=%wide.region_2.6_spmd.clone.sunk | while | flops 571539712 | bytes 104504224 | solution.py:92
  147.3 8.0 %multiply_sqrt_fusion.2 = (f32[32,4,128]{1,2,0:T(8,128)S(1)}, f32[32,4,128]{1,2,0:T(8,128)S(1)}) fusion(f32[4]{0:T(128)S(1)} %multiply_add_fusion.2, f32[32,128]{1,0:T(8,128)S(1)} %bitcast.132, pred[128]{0:T(512)(128)(4,1)S(1)} %iota_compare_fusion.10), kind=kLoop, calls=%fused_computation.6.clone.1 | loop fusion | flops 32768 | bytes 147600 | tf_op jit(solution)/shard_map/while/body/eval_jaxpr/sqrt | solution.py:77
  155.3 7.1 %div.64 = f32[32,4,128,128]{2,1,3,0:T(4,128)} broadcast(f32[32,4,128]{1,2,0:T(8,128)S(1)} %get-tuple-element.168), dimensions={0,1,3} | broadcast | bytes 8454144 | tf_op jit(solution)/shard_map/while/body/eval_jaxpr/div | solution.py:77
  162.5 10.3 %div.65 = f32[32,512,128]{1,2,0:T(8,128)} reshape(f32[32,4,128,128]{2,1,3,0:T(4,128)} %div.64) | data formatting | bytes 16777216 | tf_op jit(solution)/shard_map/while/body/eval_jaxpr/div | solution.py:77
  172.8 7.0 %mul.237 = f32[32,4,128,128]{2,1,3,0:T(4,128)} broadcast(f32[32,4,128]{1,2,0:T(8,128)S(1)} %get-tuple-element.167), dimensions={0,1,3} | broadcast | bytes 8454144 | tf_op jit(solution)/shard_map/while/body/eval_jaxpr/mul | solution.py:80
  179.8 10.3 %mul.238 = f32[32,512,128]{1,2,0:T(8,128)} reshape(f32[32,4,128,128]{2,1,3,0:T(4,128)} %mul.237) | data formatting | bytes 16777216 | tf_op jit(solution)/shard_map/while/body/eval_jaxpr/mul | solution.py:80
  190.1 1.3 fusion.86
  191.6 10.1 %multiply_convert_fusion.2 = bf16[32,512,128]{1,2,0:T(8,128)(2,1)} fusion(f32[32,512,128]{1,2,0:T(8,128)} %mul.238, f32[32,512,128]{1,2,0:T(8,128)} %div.65, f32[512,128]{0,1:T(8,128)S(1)} %bitcast.125), kind=kLoop, calls=%fused_computation.3.clone.1 | loop fusion | flops 6291456 | bytes 21233664 | tf_op jit(solution)/shard_map/while/body/eval_jaxpr/convert_element_type | solution.py:80
  201.7 1.4 fusion.89
  203.3 4.9 %multiply_reduce_fusion.3 = f32[32,512]{1,0:T(8,128)S(1)} fusion(bf16[32,512,128]{1,2,0:T(8,128)(2,1)} %multiply_convert_fusion.2, bf16[1,128,128]{1,2,0:T(8,128)(2,1)S(1)} %copy.79), kind=kOutput, calls=%fused_computation.2.clone.1 | convolution fusion | flops 543145984 | bytes 4292608 | tf_op jit(solution)/shard_map/while/body/eval_jaxpr/fcm,mn->fcn/dot_general | solution.py:86
  208.1 1.3 fusion.87
  213.3 8.0 %multiply_sqrt_fusion.2 = (f32[32,4,128]{1,2,0:T(8,128)S(1)}, f32[32,4,128]{1,2,0:T(8,128)S(1)}) fusion(f32[4]{0:T(128)S(1)} %multiply_add_fusion.2, f32[32,128]{1,0:T(8,128)S(1)} %bitcast.132, pred[128]{0:T(512)(128)(4,1)S(1)} %iota_compare_fusion.10), kind=kLoop, calls=%fused_computation.6.clone.1 | loop fusion | flops 32768 | bytes 147600 | tf_op jit(solution)/shard_map/while/body/eval_jaxpr/sqrt | solution.py:77
  221.3 7.1 %div.64 = f32[32,4,128,128]{2,1,3,0:T(4,128)} broadcast(f32[32,4,128]{1,2,0:T(8,128)S(1)} %get-tuple-element.168), dimensions={0,1,3} | broadcast | bytes 8454144 | tf_op jit(solution)/shard_map/while/body/eval_jaxpr/div | solution.py:77
  228.5 10.3 %div.65 = f32[32,512,128]{1,2,0:T(8,128)} reshape(f32[32,4,128,128]{2,1,3,0:T(4,128)} %div.64) | data formatting | bytes 16777216 | tf_op jit(solution)/shard_map/while/body/eval_jaxpr/div | solution.py:77
  238.7 7.0 %mul.237 = f32[32,4,128,128]{2,1,3,0:T(4,128)} broadcast(f32[32,4,128]{1,2,0:T(8,128)S(1)} %get-tuple-element.167), dimensions={0,1,3} | broadcast | bytes 8454144 | tf_op jit(solution)/shard_map/while/body/eval_jaxpr/mul | solution.py:80
  245.8 10.3 %mul.238 = f32[32,512,128]{1,2,0:T(8,128)} reshape(f32[32,4,128,128]{2,1,3,0:T(4,128)} %mul.237) | data formatting | bytes 16777216 | tf_op jit(solution)/shard_map/while/body/eval_jaxpr/mul | solution.py:80
  257.6 10.1 %multiply_convert_fusion.2 = bf16[32,512,128]{1,2,0:T(8,128)(2,1)} fusion(f32[32,512,128]{1,2,0:T(8,128)} %mul.238, f32[32,512,128]{1,2,0:T(8,128)} %div.65, f32[512,128]{0,1:T(8,128)S(1)} %bitcast.125), kind=kLoop, calls=%fused_computation.3.clone.1 | loop fusion | flops 6291456 | bytes 21233664 | tf_op jit(solution)/shard_map/while/body/eval_jaxpr/convert_element_type | solution.py:80
  267.7 1.4 fusion.89
  269.3 4.9 %multiply_reduce_fusion.3 = f32[32,512]{1,0:T(8,128)S(1)} fusion(bf16[32,512,128]{1,2,0:T(8,128)(2,1)} %multiply_convert_fusion.2, bf16[1,128,128]{1,2,0:T(8,128)(2,1)S(1)} %copy.79), kind=kOutput, calls=%fused_computation.2.clone.1 | convolution fusion | flops 543145984 | bytes 4292608 | tf_op jit(solution)/shard_map/while/body/eval_jaxpr/fcm,mn->fcn/dot_general | solution.py:86
  274.1 1.3 fusion.87
  279.3 8.0 %multiply_sqrt_fusion.2 = (f32[32,4,128]{1,2,0:T(8,128)S(1)}, f32[32,4,128]{1,2,0:T(8,128)S(1)}) fusion(f32[4]{0:T(128)S(1)} %multiply_add_fusion.2, f32[32,128]{1,0:T(8,128)S(1)} %bitcast.132, pred[128]{0:T(512)(128)(4,1)S(1)} %iota_compare_fusion.10), kind=kLoop, calls=%fused_computation.6.clone.1 | loop fusion | flops 32768 | bytes 147600 | tf_op jit(solution)/shard_map/while/body/eval_jaxpr/sqrt | solution.py:77
  287.3 7.1 %div.64 = f32[32,4,128,128]{2,1,3,0:T(4,128)} broadcast(f32[32,4,128]{1,2,0:T(8,128)S(1)} %get-tuple-element.168), dimensions={0,1,3} | broadcast | bytes 8454144 | tf_op jit(solution)/shard_map/while/body/eval_jaxpr/div | solution.py:77
  294.5 10.3 %div.65 = f32[32,512,128]{1,2,0:T(8,128)} reshape(f32[32,4,128,128]{2,1,3,0:T(4,128)} %div.64) | data formatting | bytes 16777216 | tf_op jit(solution)/shard_map/while/body/eval_jaxpr/div | solution.py:77
  304.7 7.0 %mul.237 = f32[32,4,128,128]{2,1,3,0:T(4,128)} broadcast(f32[32,4,128]{1,2,0:T(8,128)S(1)} %get-tuple-element.167), dimensions={0,1,3} | broadcast | bytes 8454144 | tf_op jit(solution)/shard_map/while/body/eval_jaxpr/mul | solution.py:80
  311.8 10.3 %mul.238 = f32[32,512,128]{1,2,0:T(8,128)} reshape(f32[32,4,128,128]{2,1,3,0:T(4,128)} %mul.237) | data formatting | bytes 16777216 | tf_op jit(solution)/shard_map/while/body/eval_jaxpr/mul | solution.py:80
  322.1 1.3 fusion.86
  323.6 10.1 %multiply_convert_fusion.2 = bf16[32,512,128]{1,2,0:T(8,128)(2,1)} fusion(f32[32,512,128]{1,2,0:T(8,128)} %mul.238, f32[32,512,128]{1,2,0:T(8,128)} %div.65, f32[512,128]{0,1:T(8,128)S(1)} %bitcast.125), kind=kLoop, calls=%fused_computation.3.clone.1 | loop fusion | flops 6291456 | bytes 21233664 | tf_op jit(solution)/shard_map/while/body/eval_jaxpr/convert_element_type | solution.py:80
  333.7 1.4 fusion.89
  335.3 4.9 %multiply_reduce_fusion.3 = f32[32,512]{1,0:T(8,128)S(1)} fusion(bf16[32,512,128]{1,2,0:T(8,128)(2,1)} %multiply_convert_fusion.2, bf16[1,128,128]{1,2,0:T(8,128)(2,1)S(1)} %copy.79), kind=kOutput, calls=%fused_computation.2.clone.1 | convolution fusion | flops 543145984 | bytes 4292608 | tf_op jit(solution)/shard_map/while/body/eval_jaxpr/fcm,mn->fcn/dot_general | solution.py:86
  340.1 1.3 fusion.87
  345.3 8.0 %multiply_sqrt_fusion.2 = (f32[32,4,128]{1,2,0:T(8,128)S(1)}, f32[32,4,128]{1,2,0:T(8,128)S(1)}) fusion(f32[4]{0:T(128)S(1)} %multiply_add_fusion.2, f32[32,128]{1,0:T(8,128)S(1)} %bitcast.132, pred[128]{0:T(512)(128)(4,1)S(1)} %iota_compare_fusion.10), kind=kLoop, calls=%fused_computation.6.clone.1 | loop fusion | flops 32768 | bytes 147600 | tf_op jit(solution)/shard_map/while/body/eval_jaxpr/sqrt | solution.py:77
  353.3 7.1 %div.64 = f32[32,4,128,128]{2,1,3,0:T(4,128)} broadcast(f32[32,4,128]{1,2,0:T(8,128)S(1)} %get-tuple-element.168), dimensions={0,1,3} | broadcast | bytes 8454144 | tf_op jit(solution)/shard_map/while/body/eval_jaxpr/div | solution.py:77
  360.5 10.3 %div.65 = f32[32,512,128]{1,2,0:T(8,128)} reshape(f32[32,4,128,128]{2,1,3,0:T(4,128)} %div.64) | data formatting | bytes 16777216 | tf_op jit(solution)/shard_map/while/body/eval_jaxpr/div | solution.py:77
  370.7 7.0 %mul.237 = f32[32,4,128,128]{2,1,3,0:T(4,128)} broadcast(f32[32,4,128]{1,2,0:T(8,128)S(1)} %get-tuple-element.167), dimensions={0,1,3} | broadcast | bytes 8454144 | tf_op jit(solution)/shard_map/while/body/eval_jaxpr/mul | solution.py:80
  377.8 10.3 %mul.238 = f32[32,512,128]{1,2,0:T(8,128)} reshape(f32[32,4,128,128]{2,1,3,0:T(4,128)} %mul.237) | data formatting | bytes 16777216 | tf_op jit(solution)/shard_map/while/body/eval_jaxpr/mul | solution.py:80
  388.1 1.3 fusion.86
  389.6 10.1 %multiply_convert_fusion.2 = bf16[32,512,128]{1,2,0:T(8,128)(2,1)} fusion(f32[32,512,128]{1,2,0:T(8,128)} %mul.238, f32[32,512,128]{1,2,0:T(8,128)} %div.65, f32[512,128]{0,1:T(8,128)S(1)} %bitcast.125), kind=kLoop, calls=%fused_computation.3.clone.1 | loop fusion | flops 6291456 | bytes 21233664 | tf_op jit(solution)/shard_map/while/body/eval_jaxpr/convert_element_type | solution.py:80
  399.7 1.4 fusion.89
  401.2 4.9 %multiply_reduce_fusion.3 = f32[32,512]{1,0:T(8,128)S(1)} fusion(bf16[32,512,128]{1,2,0:T(8,128)(2,1)} %multiply_convert_fusion.2, bf16[1,128,128]{1,2,0:T(8,128)(2,1)S(1)} %copy.79), kind=kOutput, calls=%fused_computation.2.clone.1 | convolution fusion | flops 543145984 | bytes 4292608 | tf_op jit(solution)/shard_map/while/body/eval_jaxpr/fcm,mn->fcn/dot_general | solution.py:86
  406.1 1.3 fusion.87
  408.3 30.2 %psum.15 = f32[16,128]{1,0:T(8,128)S(1)} all-reduce(f32[16,128]{1,0:T(8,128)S(1)} %bitcast.134), channel_id=1, replica_groups=mesh['groups'=2,'chan'=16] {'chan'}, use_global_device_ids=true, to_apply=%region_7.8 | all-reduce | flops 2048 | bytes 16384 | tf_op jit(solution)/shard_map/psum | solution.py:133
  (117 shorter events, 23.0 us)
Async XLA Ops:
  6.5 50.4 %copy-start = (f32[8,64,512]{2,1,0:T(8,128)S(1)}, f32[8,64,512]{2,1,0:T(8,128)}, u32[]{:S(2)}) copy-start(f32[8,64,512]{2,1,0:T(8,128)} %param.13) | copy-start | bytes 3145732
  6.5 131.4 %all-gather.2.cloned.1.call-start = ((), (), s32[]{:S(2)}) async-start(), calls=%async_computation.1 | async-start | bytes 4456448 | tf_op jit(solution)/shard_map/all_gather | solution.py:110
  7.3 35.6 %copy-start.8 = (bf16[2,256,4096]{2,1,0:T(8,128)(2,1)S(1)}, bf16[2,256,4096]{2,1,0:T(8,128)(2,1)}, u32[]{:S(2)}) copy-start(bf16[2,256,4096]{2,1,0:T(8,128)(2,1)} %param.9) | copy-start | bytes 12582916
  47.4 9.8 %copy-start.6 = (f32[8,64,128]{2,1,0:T(8,128)S(1)}, f32[8,64,128]{2,1,0:T(8,128)}, u32[]{:S(2)}) copy-start(f32[8,64,128]{2,1,0:T(8,128)} %param.14) | copy-start | bytes 786436
  47.4 10.0 %copy-start.5 = (bf16[8,64,256]{2,1,0:T(8,128)(2,1)S(1)}, bf16[8,64,256]{2,1,0:T(8,128)(2,1)}, u32[]{:S(2)}) copy-start(bf16[8,64,256]{2,1,0:T(8,128)(2,1)} %param.11) | copy-start | bytes 786436
  47.4 86.5 %copy-start.7 = (s32[8]{0:T(128)S(1)}, s32[8]{0:T(128)}, u32[]{:S(2)}) copy-start(s32[8]{0:T(128)} %param.12) | copy-start | bytes 100
  49.5 85.7 %all-to-all-start = ((bf16[2,512,2,256]{3,2,0,1:T(2,128)(2,1)}), bf16[2,512,2,256]{3,2,0,1:T(2,128)(2,1)S(1)}, u32[]{:S(2)}, u32[]{:S(2)}) async-start(bf16[2,512,2,256]{3,2,0,1:T(2,128)(2,1)} %copy.25), calls=%async_computation | async-start | bytes 2097152 | tf_op jit(solution)/shard_map/all_to_all | solution.py:108
  137.9 6.4 %copy-start.9 = (s32[4]{0:T(128)S(1)}, s32[4]{0:T(128)}, u32[]{:S(2)}) copy-start(s32[4]{0:T(128)} %param.15) | copy-start | bytes 52
  191.6 10.1 %copy-start.3 = (f32[8,128,128]{2,1,0:T(8,128)S(1)}, f32[8,128,128]{2,1,0:T(8,128)}, u32[]{:S(2)}) copy-start(f32[8,128,128]{2,1,0:T(8,128)} %get-tuple-element.199) | copy-start | bytes 1572868 | tf_op jit(solution)/shard_map/while
  201.7 6.4 %copy-start.4 = (f32[8,32,4,128]{3,2,1,0:T(4,128)S(1)}, f32[8,32,4,128]{3,2,1,0:T(4,128)}, u32[]{:S(2)}) copy-start(f32[8,32,4,128]{3,2,1,0:T(4,128)} %get-tuple-element.194) | copy-start | bytes 1572868 | tf_op jit(solution)/shard_map/while
  203.3 6.2 %copy-start.2 = (bf16[32,512,128]{1,2,0:T(8,128)(2,1)S(1)}, bf16[32,512,128]{1,2,0:T(8,128)(2,1)}, u32[]{:S(2)}) copy-start(bf16[32,512,128]{1,2,0:T(8,128)(2,1)} %multiply_convert_fusion.2) | copy-start | bytes 12582916 | tf_op jit(solution)/shard_map/while
  257.6 10.1 %copy-start.3 = (f32[8,128,128]{2,1,0:T(8,128)S(1)}, f32[8,128,128]{2,1,0:T(8,128)}, u32[]{:S(2)}) copy-start(f32[8,128,128]{2,1,0:T(8,128)} %get-tuple-element.199) | copy-start | bytes 1572868 | tf_op jit(solution)/shard_map/while
  267.7 6.4 %copy-start.4 = (f32[8,32,4,128]{3,2,1,0:T(4,128)S(1)}, f32[8,32,4,128]{3,2,1,0:T(4,128)}, u32[]{:S(2)}) copy-start(f32[8,32,4,128]{3,2,1,0:T(4,128)} %get-tuple-element.194) | copy-start | bytes 1572868 | tf_op jit(solution)/shard_map/while
  269.2 6.2 %copy-start.2 = (bf16[32,512,128]{1,2,0:T(8,128)(2,1)S(1)}, bf16[32,512,128]{1,2,0:T(8,128)(2,1)}, u32[]{:S(2)}) copy-start(bf16[32,512,128]{1,2,0:T(8,128)(2,1)} %multiply_convert_fusion.2) | copy-start | bytes 12582916 | tf_op jit(solution)/shard_map/while
  323.6 10.1 %copy-start.3 = (f32[8,128,128]{2,1,0:T(8,128)S(1)}, f32[8,128,128]{2,1,0:T(8,128)}, u32[]{:S(2)}) copy-start(f32[8,128,128]{2,1,0:T(8,128)} %get-tuple-element.199) | copy-start | bytes 1572868 | tf_op jit(solution)/shard_map/while
  333.7 6.4 %copy-start.4 = (f32[8,32,4,128]{3,2,1,0:T(4,128)S(1)}, f32[8,32,4,128]{3,2,1,0:T(4,128)}, u32[]{:S(2)}) copy-start(f32[8,32,4,128]{3,2,1,0:T(4,128)} %get-tuple-element.194) | copy-start | bytes 1572868 | tf_op jit(solution)/shard_map/while
  335.2 6.2 %copy-start.2 = (bf16[32,512,128]{1,2,0:T(8,128)(2,1)S(1)}, bf16[32,512,128]{1,2,0:T(8,128)(2,1)}, u32[]{:S(2)}) copy-start(bf16[32,512,128]{1,2,0:T(8,128)(2,1)} %multiply_convert_fusion.2) | copy-start | bytes 12582916 | tf_op jit(solution)/shard_map/while
  389.6 10.1 %copy-start.3 = (f32[8,128,128]{2,1,0:T(8,128)S(1)}, f32[8,128,128]{2,1,0:T(8,128)}, u32[]{:S(2)}) copy-start(f32[8,128,128]{2,1,0:T(8,128)} %get-tuple-element.199) | copy-start | bytes 1572868 | tf_op jit(solution)/shard_map/while
  399.7 6.4 %copy-start.4 = (f32[8,32,4,128]{3,2,1,0:T(4,128)S(1)}, f32[8,32,4,128]{3,2,1,0:T(4,128)}, u32[]{:S(2)}) copy-start(f32[8,32,4,128]{3,2,1,0:T(4,128)} %get-tuple-element.194) | copy-start | bytes 1572868 | tf_op jit(solution)/shard_map/while
  401.2 6.2 %copy-start.2 = (bf16[32,512,128]{1,2,0:T(8,128)(2,1)S(1)}, bf16[32,512,128]{1,2,0:T(8,128)(2,1)}, u32[]{:S(2)}) copy-start(bf16[32,512,128]{1,2,0:T(8,128)(2,1)} %multiply_convert_fusion.2) | copy-start | bytes 12582916 | tf_op jit(solution)/shard_map/while
  408.3 32.1 %copy-start.1 = (f32[8,64,512]{2,1,0:T(8,128)S(1)}, f32[8,64,512]{2,1,0:T(8,128)}, u32[]{:S(2)}) copy-start(f32[8,64,512]{2,1,0:T(8,128)} %param.13) | copy-start | bytes 3145732
Sparse Core Ops, SparseCore 0:
  9.5 64.8 all-gather.1
where the time goes:
time: 449 us; the launch traced here: 447 us
  local copies, waits for them, and re-layouts  151 us (34%)
  other arithmetic  114 us (25%)
  blocking collectives  106 us (24%)
  matrix products  50.9 us (11%)
  between operations  13.6 us (3%)
  starting transfers between devices  7.39 us (2%)
    psum x1, blocking collectives, per_device(): gram = lax.psum(local_gram.reshape(segs, modes * modes), 'chan')  75.9 us
    div x12, local copies, waits for them, and re-layouts, one_block(): amplitude = mode_block[None, None, :, :] / jnp.sqrt(phases)[:, :, None, :]  69.8 us
    mul x8, local copies, waits for them, and re-layouts, one_block(): amplitude * trig[:, :, None, :]  69.3 us
    convert_element_type x4, other arithmetic, one_block(): (amplitude * trig[:, :, None, :]).reshape(freqs, cells, 2 * modes)  40.5 us
    another operation x1, other arithmetic  35.6 us
    sqrt x4, other arithmetic, one_block(): amplitude = mode_block[None, None, :, :] / jnp.sqrt(phases)[:, :, None, :]  32 us
    psum x1, blocking collectives, per_device(): total_surface = lax.psum(partial_surface, 'chan')  30.2 us
    dot_general x4, matrix products, one_block(): jnp.einsum('fcm,mn->fcn', replica, gram_block, preferred_element_type=jnp...  19.4 us
  transfers between devices with their start and end apart: 2, of which 0 were waited for; matrix products, arithmetic and copies ran while one was open for 10% of the time, Pallas kernels for 0%

commit v1 on v0

--- a/solution.py
+++ b/solution.py
@@ -1,6 +1,11 @@
+import functools
+import math
+
 import jax
 import jax.numpy as jnp
 from jax import lax
+from jax.experimental import pallas as pl
+from jax.experimental.pallas import tpu as pltpu
 from jax.sharding import PartitionSpec as P
 
 F = 512
@@ -93,7 +98,7 @@
     return parts.reshape(blocks * ranges_per_block, depths)
 
 
-def per_device(
+def per_device_plain(
     snapshots, freq_bins, mode_shapes, mode_counts, wavenumbers, source_modes, segment_owner
 ):
     devices_chan = lax.axis_size("chan")
@@ -138,6 +143,457 @@
     return own_surface / highest_value
 
 
+LANES = 128
+MESH = pl.DeviceIdType.MESH
+HIGHEST = lax.Precision.HIGHEST
+
+
+def sincos_small(x):
+    y = x * x
+    sine = x + x * y * (
+        -1.6666667e-1 + y * (8.3333333e-3 + y * (-1.9841270e-4 + y * 2.7557319e-6))
+    )
+    cosine = 1.0 + y * (
+        -0.5 + y * (4.1666667e-2 + y * (-1.3888889e-3 + y * (2.4801587e-5 - y * 2.7557319e-7)))
+    )
+    return sine, cosine
+
+
+def turn(quadrant, sine, cosine):
+    odd = (quadrant & 1) == 1
+    c = jnp.where(odd, sine, cosine)
+    s = jnp.where(odd, cosine, sine)
+    return (
+        jnp.where((quadrant & 2) != 0, -s, s),
+        jnp.where(((quadrant + 1) & 2) != 0, -c, c),
+    )
+
+
+def sincos_bins(q, samples):
+    quarter = samples // 4
+    q = q & (samples - 1)
+    quadrant = (q + quarter // 2) // quarter
+    x = (q - quadrant * quarter).astype(jnp.float32) * (2.0 * math.pi / samples)
+    return turn(quadrant, *sincos_small(x))
+
+
+def sincos_wide(x):
+    n = jnp.floor(x * (2.0 / math.pi) + 0.5)
+    y = ((x - n * 1.5703125) - n * 4.837512969970703125e-4) - n * 7.54978995489188216e-8
+    return turn(n.astype(jnp.int32), *sincos_small(y))
+
+
+def fused_kernel(
+    devices,
+    freq_ref,
+    snaps_hbm,
+    modes_ref,
+    phases_ref,
+    source_ref,
+    out_ref,
+    snaps,
+    table,
+    cos_a,
+    sin_a,
+    cos_b,
+    sin_b,
+    proj_send,
+    proj_recv,
+    trace_send,
+    trace_recv,
+    gram_part,
+    gram_recv,
+    gram_own,
+    gram_full,
+    terms_a,
+    terms_b,
+    surf_own,
+    surf_recv,
+    total_ref,
+    load_sem,
+    proj_ssem,
+    proj_rsem,
+    trace_ssem,
+    trace_rsem,
+    gram_ssem,
+    gram_rsem,
+    full_ssem,
+    full_rsem,
+    surf_ssem,
+    surf_rsem,
+):
+    me = lax.axis_index("chan")
+    snap_count, channels, samples = snaps_hbm.shape
+    blocks, modes, depths = source_ref.shape
+    columns = freq_ref.shape[1]
+    width = table.shape[1]
+    f32 = jnp.float32
+
+    barrier = pltpu.get_barrier_semaphore()
+    for step in range(1, devices):
+        pl.semaphore_signal(
+            barrier, inc=1, device_id={"chan": (me + step) % devices}, device_id_type=MESH
+        )
+    load = pltpu.make_async_copy(snaps_hbm, snaps, load_sem)
+    load.start()
+
+    def send(src, dst, ssem, rsem, peer):
+        return pltpu.make_async_remote_copy(
+            src_ref=src,
+            dst_ref=dst,
+            send_sem=ssem,
+            recv_sem=rsem,
+            device_id={"chan": peer},
+            device_id_type=MESH,
+        )
+
+    shapes = modes_ref[...]
+    inner = lax.dot_general(shapes, shapes, (((1,), (1,)), ((), ())), preferred_element_type=f32)
+    low_half = lax.broadcasted_iota(jnp.int32, (modes, LANES), 1) < modes
+    for pair in range(blocks // 2):
+        base = pair * LANES
+        gram_part[pair * modes : (pair + 1) * modes, :] = jnp.where(
+            low_half,
+            inner[base : base + modes, base : base + LANES],
+            inner[base + modes : base + LANES, base : base + LANES],
+        )
+    pl.semaphore_wait(barrier, devices - 1)
+
+    @pl.loop(1, devices)
+    def _(step):
+        peer = (me + step) % devices
+        send(
+            gram_part.at[pl.ds(pl.multiple_of(peer * 8, 8), 8), :],
+            gram_recv.at[me],
+            gram_ssem.at[peer],
+            gram_rsem.at[me],
+            peer,
+        ).start()
+
+    gram_recv[me] = gram_part[pl.ds(pl.multiple_of(me * 8, 8), 8), :]
+
+    half = cos_a.shape[0]
+    freqs = freq_ref[...]
+    column = lax.broadcasted_iota(jnp.int32, (half, columns), 1)
+    row = lax.broadcasted_iota(jnp.int32, (half, columns), 0)
+    part_size = columns // devices // 2
+    shift = ((column // part_size) & 1) * (samples // 4)
+    sin_v, cos_v = sincos_bins(freqs * (row * half) + shift, samples)
+    sin_a[...] = sin_v
+    cos_a[...] = cos_v
+    sin_v, cos_v = sincos_bins(freqs * row, samples)
+    sin_b[...] = sin_v
+    cos_b[...] = cos_v
+
+    @pl.loop(1, devices)
+    def _(step):
+        peer = (me + step) % devices
+        send(
+            gram_part.at[pl.ds(0, 8), :],
+            gram_recv.at[peer],
+            gram_ssem.at[peer],
+            gram_rsem.at[peer],
+            peer,
+        ).wait_recv()
+
+    gram_own[...] = jnp.sum(gram_recv[...], axis=0)
+    own_rows = pl.ds(pl.multiple_of(me * 8, 8), 8)
+    gram_full[own_rows, :] = gram_own[...]
+
+    @pl.loop(1, devices)
+    def _(step):
+        peer = (me + step) % devices
+        send(
+            gram_own, gram_full.at[own_rows, :], full_ssem.at[peer], full_rsem.at[me], peer
+        ).start()
+
+    load.wait()
+    per_chunk = width // (columns // devices)
+    chunk_count = columns // width
+    wide_low = lax.broadcasted_iota(jnp.int32, (blocks * modes, LANES), 1) < LANES // 2
+    thin_low = wide_low[:8]
+
+    @pl.loop(0, chunk_count)
+    def _(step):
+        chunk = (me // per_chunk + 1 + step) % chunk_count
+        cols = pl.ds(pl.multiple_of(chunk * width, width), width)
+        cb = cos_b[:, cols]
+        sb = sin_b[:, cols]
+
+        @pl.loop(0, half, unroll=4)
+        def _(a):
+            ca = cos_a[pl.ds(a, 1), cols]
+            sa = sin_a[pl.ds(a, 1), cols]
+            table[pl.ds(pl.multiple_of(a * half, half), half), :] = (ca * cb - sa * sb).astype(
+                jnp.bfloat16
+            )
+
+        parts = []
+        sums = []
+        for snap in range(snap_count):
+            spectra = jnp.dot(snaps[snap], table[...], preferred_element_type=f32).astype(
+                jnp.bfloat16
+            )
+            wide = spectra.astype(f32)
+            sums.append(jnp.broadcast_to(jnp.sum(wide * wide, axis=0, keepdims=True), (8, width)))
+            parts.append(jnp.dot(shapes, spectra, preferred_element_type=f32))
+        for pair in range(per_chunk // 2):
+            lanes = slice(pair * LANES, (pair + 1) * LANES)
+            p0, p1 = parts[0][:, lanes], parts[1][:, lanes]
+            t0, t1 = sums[0][:, lanes], sums[1][:, lanes]
+            for side in range(2):
+                dest = chunk * per_chunk + 2 * pair + side
+                if side == 0:
+                    message = jnp.where(wide_low, p0, pltpu.roll(p1, LANES // 2, 1))
+                    trace = jnp.where(thin_low, t0, pltpu.roll(t1, LANES // 2, 1))
+                else:
+                    message = jnp.where(wide_low, pltpu.roll(p0, LANES // 2, 1), p1)
+                    trace = jnp.where(thin_low, pltpu.roll(t0, LANES // 2, 1), t1)
+                proj_send[dest] = message.astype(jnp.bfloat16)
+                trace_send[dest] = trace
+
+                @pl.when(dest != me)
+                def _():
+                    send(
+                        proj_send.at[dest],
+                        proj_recv.at[me],
+                        proj_ssem.at[dest],
+                        proj_rsem.at[me],
+                        dest,
+                    ).start()
+                    send(
+                        trace_send.at[dest],
+                        trace_recv.at[me],
+                        trace_ssem.at[dest],
+                        trace_rsem.at[me],
+                        dest,
+                    ).start()
+
+    proj_recv[me] = proj_send[me]
+    trace_recv[me] = trace_send[me]
+
+    @pl.loop(1, devices)
+    def _(step):
+        peer = (me + step) % devices
+        send(
+            gram_own,
+            gram_full.at[pl.ds(pl.multiple_of(peer * 8, 8), 8), :],
+            full_ssem.at[peer],
+            full_rsem.at[peer],
+            peer,
+        ).wait_recv()
+
+    gram = gram_full[...].astype(jnp.bfloat16).astype(f32)
+    waves_sin = []
+    waves_cos = []
+    norms = []
+    for block in range(blocks):
+        phases = phases_ref[block]
+        sine, cosine = sincos_wide(phases)
+        scale = 1.0 / jnp.sqrt(phases)
+        sine, cosine = sine * scale, cosine * scale
+        waves_sin.append(sine)
+        waves_cos.append(cosine)
+        source = source_ref[block]
+        rows = slice((block // 2) * modes, (block // 2 + 1) * modes)
+        for m in range(modes):
+            lane = (block % 2) * modes + m
+            at = slice(m * modes, (m + 1) * modes)
+            terms_a[at, :] = (cosine[m : m + 1] * cosine + sine[m : m + 1] * sine).astype(
+                jnp.bfloat16
+            )
+            terms_b[at, :] = (
+                gram[rows, lane : lane + 1] * (source[m : m + 1] * source)
+            ).astype(jnp.bfloat16)
+        norms.append(
+            lax.dot_general(
+                terms_a[...],
+                terms_b[...],
+                (((0,), (0,)), ((), ())),
+                preferred_element_type=f32,
+            )
+        )
+
+    @pl.loop(1, devices)
+    def _(step):
+        peer = (me + step) % devices
+        send(
+            proj_send.at[peer], proj_recv.at[peer], proj_ssem.at[peer], proj_rsem.at[peer], peer
+        ).wait_recv()
+        send(
+            trace_send.at[peer],
+            trace_recv.at[peer],
+            trace_ssem.at[peer],
+            trace_rsem.at[peer],
+            peer,
+        ).wait_recv()
+
+    proj = proj_recv[0].astype(f32)
+    for source_id in range(1, devices):
+        proj = proj + proj_recv[source_id].astype(f32)
+    proj = proj.astype(jnp.bfloat16)
+    trace = jnp.sum(trace_recv[...], axis=0)
+    quarter = LANES // 4
+    trace = trace + pltpu.roll(trace, 2 * quarter, 1)
+    trace = trace + pltpu.roll(trace, quarter, 1)
+    level = (1.0 / jnp.sqrt(snap_count * trace))[:1]
+
+    pick_in = lax.broadcasted_iota(jnp.int32, (LANES, 4 * LANES), 0)
+    pick_out = lax.broadcasted_iota(jnp.int32, (LANES, 4 * LANES), 1)
+    pick = (pick_in // quarter == pick_out // LANES) & (pick_in % quarter == pick_out % quarter)
+    spread = jnp.dot(proj, pick.astype(f32).astype(jnp.bfloat16), preferred_element_type=f32)
+    for block in range(blocks):
+        sine, cosine = waves_sin[block] * level, waves_cos[block] * level
+        rows = slice(block * modes, (block + 1) * modes)
+        coupled = []
+        for snap in range(snap_count):
+            real = spread[rows, (2 * snap) * LANES : (2 * snap + 1) * LANES]
+            imag = spread[rows, (2 * snap + 1) * LANES : (2 * snap + 2) * LANES]
+            coupled.append(cosine * real + sine * imag)
+            coupled.append(cosine * imag - sine * real)
+        coupled = jnp.concatenate(coupled, axis=1)
+        coupled_high = coupled.astype(jnp.bfloat16)
+        coupled_low = (coupled - coupled_high.astype(f32)).astype(jnp.bfloat16)
+        source = source_ref[block]
+        source_high = source.astype(jnp.bfloat16)
+        source_low = (source - source_high.astype(f32)).astype(jnp.bfloat16)
+        beams = lax.dot_general(
+            jnp.concatenate([coupled_high, coupled_low, coupled_high], axis=0),
+            jnp.concatenate([source_high, source_high, source_low], axis=0),
+            (((0,), (0,)), ((), ())),
+            preferred_element_type=f32,
+        )
+        squares = beams * beams
+        power = (
+            squares[:LANES]
+            + squares[LANES : 2 * LANES]
+            + squares[2 * LANES : 3 * LANES]
+            + squares[3 * LANES :]
+        )
+        ratio = power / norms[block]
+        for j in range(4):
+            surf_own[block * 4 + j : block * 4 + j + 1, :] = jnp.sum(
+                ratio[j * quarter : (j + 1) * quarter], axis=0, keepdims=True
+            )
+
+    surf_recv[me] = surf_own[...]
+
+    @pl.loop(1, devices)
+    def _(step):
+        peer = (me + step) % devices
+        send(surf_own, surf_recv.at[me], surf_ssem.at[peer], surf_rsem.at[me], peer).start()
+
+    @pl.loop(1, devices)
+    def _(step):
+        peer = (me + step) % devices
+        send(surf_own, surf_recv.at[peer], surf_ssem.at[peer], surf_rsem.at[peer], peer).wait_recv()
+
+    total = jnp.sum(surf_recv[...], axis=0) / (columns // 2)
+    total_ref[...] = total
+    out_ref[...] = total_ref[pl.ds(me, 1), :] / jnp.max(total)
+
+    @pl.loop(1, devices)
+    def _(step):
+        peer = (me + step) % devices
+        send(
+            gram_part.at[pl.ds(pl.multiple_of(peer * 8, 8), 8), :],
+            gram_recv.at[me],
+            gram_ssem.at[peer],
+            gram_rsem.at[me],
+            peer,
+        ).wait_send()
+        send(
+            gram_own, gram_full.at[own_rows, :], full_ssem.at[peer], full_rsem.at[me], peer
+        ).wait_send()
+        send(
+            proj_send.at[peer], proj_recv.at[me], proj_ssem.at[peer], proj_rsem.at[me], peer
+        ).wait_send()
+        send(
+            trace_send.at[peer], trace_recv.at[me], trace_ssem.at[peer], trace_rsem.at[me], peer
+        ).wait_send()
+        send(surf_own, surf_recv.at[me], surf_ssem.at[peer], surf_rsem.at[me], peer).wait_send()
+
+
+def per_device_fused(
+    snapshots, freq_bins, mode_shapes, mode_counts, wavenumbers, source_modes, segment_owner
+):
+    devices = lax.axis_size("chan")
+    snap_count, channels, samples = snapshots.shape
+    segs, modes, depths = source_modes.shape
+    blocks = segment_owner.shape[0]
+    freqs = freq_bins.shape[0]
+    local_freqs = freqs // devices
+    columns = 2 * freqs
+    half = math.isqrt(samples)
+    freq_columns = jnp.broadcast_to(
+        freq_bins.reshape(devices, 1, local_freqs), (devices, 2, local_freqs)
+    ).reshape(1, columns)
+    shapes = jnp.take(mode_shapes, segment_owner, axis=0).reshape(blocks * modes, channels)
+    active = jnp.arange(modes, dtype=jnp.int32)[None, :] < mode_counts[:, None]
+    masked = jnp.take(source_modes * active[:, :, None], segment_owner, axis=0)
+    first_freq = lax.axis_index("chan") * local_freqs
+    waves = lax.dynamic_slice_in_dim(wavenumbers, first_freq, local_freqs, 2)
+    waves = jnp.take(waves, segment_owner, axis=0)
+    ranges = range_start + range_step * jnp.arange(blocks * RPB, dtype=jnp.float32)
+    phases = waves[:, :, None, :] * ranges.reshape(blocks, 1, RPB, 1)
+    phases = phases.reshape(blocks, modes, RPB * local_freqs)
+    f32, bf16 = jnp.float32, jnp.bfloat16
+    ranges_total = blocks * RPB
+    dma = pltpu.SemaphoreType.DMA((devices,))
+    vmem = pl.BlockSpec(memory_space=pltpu.VMEM)
+    return pl.pallas_call(
+        functools.partial(fused_kernel, devices),
+        out_shape=jax.ShapeDtypeStruct((1, depths), f32),
+        in_specs=[vmem, pl.BlockSpec(memory_space=pl.ANY), vmem, vmem, vmem],
+        out_specs=vmem,
+        scratch_shapes=[
+            pltpu.VMEM((snap_count, channels, samples), bf16),
+            pltpu.VMEM((samples, 256), bf16),
+            pltpu.VMEM((half, columns), f32),
+            pltpu.VMEM((half, columns), f32),
+            pltpu.VMEM((half, columns), f32),
+            pltpu.VMEM((half, columns), f32),
+            pltpu.VMEM((devices, blocks * modes, LANES), bf16),
+            pltpu.VMEM((devices, blocks * modes, LANES), bf16),
+            pltpu.VMEM((devices, 8, LANES), f32),
+            pltpu.VMEM((devices, 8, LANES), f32),
+            pltpu.VMEM((devices * 8, LANES), f32),
+            pltpu.VMEM((devices, 8, LANES), f32),
+            pltpu.VMEM((8, LANES), f32),
+            pltpu.VMEM((devices * 8, LANES), f32),
+            pltpu.VMEM((modes * modes, LANES), bf16),
+            pltpu.VMEM((modes * modes, LANES), bf16),
+            pltpu.VMEM((ranges_total, depths), f32),
+            pltpu.VMEM((devices, ranges_total, depths), f32),
+            pltpu.VMEM((ranges_total, depths), f32),
+            pltpu.SemaphoreType.DMA,
+        ]
+        + [dma] * 10,
+        compiler_params=pltpu.CompilerParams(
+            collective_id=0, has_side_effects=True, vmem_limit_bytes=40 * 2**20
+        ),
+    )(freq_columns, snapshots, shapes, phases, masked)
+
+
+def per_device(*args):
+    snapshots, freq_bins, mode_shapes, _, _, source_modes, segment_owner = args
+    devices = lax.axis_size("chan")
+    blocks = segment_owner.shape[0]
+    freqs = freq_bins.shape[0]
+    modes, depths = source_modes.shape[1:]
+    fits = (
+        snapshots.shape[0] == 2
+        and 2 * 2 * freqs == devices * LANES
+        and 4 * freqs // devices == LANES
+        and blocks * RPB == devices
+        and blocks * modes * modes == devices * 8 * LANES
+        and 2 * modes == LANES
+        and depths == LANES
+        and math.isqrt(snapshots.shape[2]) ** 2 == snapshots.shape[2]
+    )
+    return per_device_fused(*args) if fits else per_device_plain(*args)
+
+
 def solution(mesh):
     return jax.shard_map(
         per_device,

time: 449 us -> 58.4 us (0.13)
  local copies, waits for them, and re-layouts: 151 us -> 8.08 us
  other arithmetic: 114 us -> 3.42 us
  blocking collectives: 106 us -> 0 us
  matrix products: 50.9 us -> 0 us
  Pallas kernels: 0 us -> 46.5 us
  between operations: 13.6 us -> 0.09 us
  starting transfers between devices: 7.39 us -> 0 us
    psum x2 -> x0, blocking collectives: 106 us -> none  [the longest x1 75.9 us: per_device(): gram = lax.psum(local_gram.reshape(segs, modes * modes), 'chan')]
    div x12 -> x0, local copies, waits for them, and re-layouts: 69.8 us -> none  [one_block(): amplitude = mode_block[None, None, :, :] / jnp.sqrt(phases)[:, :, None, :]]
    mul x8 -> x4, local copies, waits for them, and re-layouts: 69.3 us -> 0.3 us  [per_device_fused(): phases = waves[:, :, None, :] * ranges.reshape(blocks, 1, RPB, 1)]
    dot_general x27 -> x0, matrix products: 50.9 us -> none  [the longest x4 19.4 us: one_block(): jnp.einsum('fcm,mn->fcn', replica, gram_block, preferred_element_type=jnp...]
    pallas_call x0 -> x1, Pallas kernels: none -> 46.5 us  [per_device_fused(): pl.pallas_call(functools.partial(fused_kernel, devices), out_shape=jax.Sh...]
    convert_element_type x7 -> x1, other arithmetic: 43.2 us -> 0.73 us  [per_device_fused(): masked = jnp.take(source_modes * active[:, :, None], segment_owner, axis=0)]
    another operation x1 -> x0, other arithmetic: 35.6 us -> none
    sqrt x4 -> x0, other arithmetic: 32 us -> none  [one_block(): amplitude = mode_block[None, None, :, :] / jnp.sqrt(phases)[:, :, None, :]]
  transfers between devices with their start and end apart: 2 -> 0, of which waited for: 0 -> 0; matrix products, arithmetic and copies ran while one was open for 10% -> 0% of each run, Pallas kernels for 0% -> 0%
where the time goes in v1:
time: 58.4 us; the launch traced here: 58.1 us
  Pallas kernels  46.5 us (80%)
  local copies, waits for them, and re-layouts  8.08 us (14%)
  other arithmetic  3.42 us (6%)
    pallas_call x1, Pallas kernels, per_device_fused(): pl.pallas_call(functools.partial(fused_kernel, devices), out_shape=jax.Sh...  46.5 us
    unnamed x5, local copies, waits for them, and re-layouts  3.93 us
    gather x1, local copies, waits for them, and re-layouts, per_device_fused(): jnp.take(mode_shapes, segment_owner, axis=0)  1.51 us

profile of v1, /device:TPU:0, one launch (start us, length us, event | category | flops | bytes accessed | tf_op | source)
XLA Modules:
  0.0 58.1 jit_solution(11192627197101583794)
XLA Ops:
  0.0 0.0 copy-start
  0.0 1.2 %copy-done = f32[8,64,512]{2,1,0:T(8,128)S(1)} copy-done((f32[8,64,512]{2,1,0:T(8,128)S(1)}, f32[8,64,512]{2,1,0:T(8,128)}, u32[]{:S(2)}) %copy-start) | copy-done | bytes 1048600
  1.2 0.1 constant_dynamic-slice_fusion
  1.4 0.7 %compare_select_fusion = s32[4]{0:T(128)S(1)} fusion(s32[4]{0:T(128)} %param.13), kind=kLoop, calls=%fused_computation.11 | loop fusion | flops 12 | bytes 32 | tf_op jit(solution)/shard_map/jit(_take)/jit(_where)/select_n | solution.py:531
  2.0 0.6 gather_fusion.1
  2.6 0.7 %compare_and_fusion = pred[4]{0:T(512)(128)(4,1)S(1)} fusion(s32[4]{0:T(128)} %param.13), kind=kLoop, calls=%fused_computation.13 | loop fusion | flops 24 | bytes 20 | tf_op jit(solution)/shard_map/jit(_take)/and | solution.py:531
  3.3 0.1 broadcast_select_fusion.1
  3.3 0.1 copy.8
  3.5 0.1 copy.9
  3.6 0.7 %fusion = f32[8,64]{1,0:T(8,128)S(1)} fusion(s32[8]{0:T(128)} %param.10), kind=kLoop, calls=%fused_computation.10 | loop fusion | flops 1024 | bytes 2080 | tf_op jit(solution)/shard_map/convert_element_type | solution.py:533
  4.3 1.1 %broadcast_multiply_fusion = f32[8,64,128]{2,1,0:T(8,128)S(1)} fusion(f32[8,64,128]{2,1,0:T(8,128)} %param.12, f32[8,64]{1,0:T(8,128)S(1)} %fusion), kind=kLoop, calls=%fused_computation.4 | loop fusion | flops 65536 | bytes 526336 | tf_op jit(solution)/shard_map/mul | solution.py:533
  5.4 0.6 gather_fusion.2
  6.0 0.1 mul.42
  6.0 0.1 mul.43
  6.1 0.1 broadcast_select_fusion
  6.2 1.5 %gather_fusion = bf16[4,64,256]{2,1,0:T(8,128)(2,1)S(1)} fusion(bf16[8,64,256]{2,1,0:T(8,128)(2,1)} %param.9, s32[1024]{0:T(1024)S(1)} %pad_clamp_fusion), kind=kCustom, calls=%fused_computation | custom fusion | bytes 262160 | tf_op jit(solution)/shard_map/jit(_take)/gather | solution.py:531
  7.7 0.1 broadcast_in_dim.49
  7.8 0.1 broadcast_in_dim.50
  7.9 0.1 bitcast_select_fusion.modes_ref
  8.0 0.8 %broadcast_in_dim.47 = s32[16,32]{1,0:T(8,128)S(1)} reshape(s32[512]{0:T(512)} %param.8) | data formatting | bytes 4096 | tf_op jit(solution)/shard_map/broadcast_in_dim | solution.py:528
  8.8 0.1 reshape.52.freq_ref
  8.9 0.0 copy-start.1
  8.9 2.2 %copy-done.1 = bf16[2,256,4096]{2,1,0:T(8,128)(2,1)S(1)} copy-done((bf16[2,256,4096]{2,1,0:T(8,128)(2,1)S(1)}, bf16[2,256,4096]{2,1,0:T(8,128)(2,1)}, u32[]{:S(2)}) %copy-start.1) | copy-done | bytes 4194328
  11.1 46.5 %shard_map.73 = f32[1,128]{1,0:T(1,128)S(1)} custom-call(s32[1,1024]{1,0:T(1,128)S(1)} %reshape.52.freq_ref, bf16[2,256,4096]{2,1,0:T(8,128)(2,1)S(1)} %copy-done.1, bf16[256,256]{1,0:T(8,128)(2,1)S(1)} %bitcast_select_fusion.modes_ref, f32[4,64,128]{2,1,0:T(8,128)S(1)} %get-tuple-element.6.phases_ref, f32[4,64,128]{2,1,0:T(8,128)S(1)} %get-tuple-element.5.source_ref), custom_call_target="tpu_custom_call" | custom-call | tf_op jit(solution)/shard_map/pallas_call | solution.py:544
  57.6 0.5 copy.11
  (4 shorter events, 0.1 us)
Async XLA Ops:
  0.0 1.2 %copy-start = (f32[8,64,512]{2,1,0:T(8,128)S(1)}, f32[8,64,512]{2,1,0:T(8,128)}, u32[]{:S(2)}) copy-start(f32[8,64,512]{2,1,0:T(8,128)} %param.11) | copy-start | bytes 3145732
  8.9 2.2 %copy-start.1 = (bf16[2,256,4096]{2,1,0:T(8,128)(2,1)S(1)}, bf16[2,256,4096]{2,1,0:T(8,128)(2,1)}, u32[]{:S(2)}) copy-start(bf16[2,256,4096]{2,1,0:T(8,128)(2,1)} %snaps_hbm.1) | copy-start | bytes 12582916

commit v2 on v1

--- a/solution.py
+++ b/solution.py
@@ -188,8 +188,10 @@
     freq_ref,
     snaps_hbm,
     modes_ref,
-    phases_ref,
-    source_ref,
+    counts_ref,
+    waves_ref,
+    modes_source_ref,
+    owner_ref,
     out_ref,
     snaps,
     table,
@@ -197,8 +199,15 @@
     sin_a,
     cos_b,
     sin_b,
-    proj_send,
-    proj_recv,
+    kept,
+    core_send,
+    core_recv,
+    side_kept,
+    side_send,
+    side_recv,
+    far_kept,
+    far_send,
+    far_recv,
     trace_send,
     trace_recv,
     gram_part,
@@ -211,8 +220,12 @@
     surf_recv,
     total_ref,
     load_sem,
-    proj_ssem,
-    proj_rsem,
+    core_ssem,
+    core_rsem,
+    side_ssem,
+    side_rsem,
+    far_ssem,
+    far_rsem,
     trace_ssem,
     trace_rsem,
     gram_ssem,
@@ -223,9 +236,17 @@
     surf_rsem,
 ):
     me = lax.axis_index("chan")
-    snap_count, channels, samples = snaps_hbm.shape
-    blocks, modes, depths = source_ref.shape
-    columns = freq_ref.shape[1]
+    snap_count = 2
+    samples = snaps_hbm.shape[1]
+    channels = snaps_hbm.shape[0] // snap_count
+    blocks = owner_ref.shape[0]
+    modes, depths = modes_source_ref.shape[1:]
+    columns = 2 * freq_ref.shape[0] * freq_ref.shape[1]
+    core = me % 2
+    side = (me // 2) % 2
+    far = me // 4
+    other_core = far * 4 + side * 2 + 1 - core
+    other_side = far * 4 + (1 - side) * 2 + core
     width = table.shape[1]
     f32 = jnp.float32
 
@@ -247,7 +268,8 @@
             device_id_type=MESH,
         )
 
-    shapes = modes_ref[...]
+    owners = [owner_ref[block] for block in range(blocks)]
+    shapes = jnp.concatenate([modes_ref[owner] for owner in owners], axis=0)
     inner = lax.dot_general(shapes, shapes, (((1,), (1,)), ((), ())), preferred_element_type=f32)
     low_half = lax.broadcasted_iota(jnp.int32, (modes, LANES), 1) < modes
     for pair in range(blocks // 2):
@@ -273,7 +295,22 @@
     gram_recv[me] = gram_part[pl.ds(pl.multiple_of(me * 8, 8), 8), :]
 
     half = cos_a.shape[0]
-    freqs = freq_ref[...]
+    lane = lax.broadcasted_iota(jnp.int32, (1, LANES), 1)
+    quarter = LANES // 4
+    group = lane // quarter
+    pieces = []
+    for piece in range(columns // LANES):
+        here = freq_ref[piece // 2 : piece // 2 + 1, :]
+        shifts = (2 * quarter, 3 * quarter, 3 * quarter, 0) if piece % 2 else (0, quarter, quarter, 2 * quarter)
+        turned = [pltpu.roll(here, n, 1) if n else here for n in shifts]
+        pieces.append(
+            jnp.where(
+                group == 0,
+                turned[0],
+                jnp.where(group == 1, turned[1], jnp.where(group == 2, turned[2], turned[3])),
+            )
+        )
+    freqs = jnp.concatenate(pieces, axis=1)
     column = lax.broadcasted_iota(jnp.int32, (half, columns), 1)
     row = lax.broadcasted_iota(jnp.int32, (half, columns), 0)
     part_size = columns // devices // 2
@@ -313,9 +350,25 @@
     wide_low = lax.broadcasted_iota(jnp.int32, (blocks * modes, LANES), 1) < LANES // 2
     thin_low = wide_low[:8]
 
-    @pl.loop(0, chunk_count)
-    def _(step):
-        chunk = (me // per_chunk + 1 + step) % chunk_count
+    def core_copy(chunk):
+        return send(
+            core_send.at[chunk], core_recv.at[chunk], core_ssem.at[chunk], core_rsem.at[chunk], other_core
+        )
+
+    def side_copy(chunk):
+        return send(
+            side_send.at[chunk], side_recv.at[chunk], side_ssem.at[chunk], side_rsem.at[chunk], other_side
+        )
+
+    def far_copy(chunk, slot):
+        peer = chunk * 4 + side * 2 + core
+        return send(far_send.at[chunk], far_recv.at[slot], far_ssem.at[chunk], far_rsem.at[slot], peer)
+
+    def chunk_of(step):
+        return (far + 1 + step) % chunk_count
+
+    def make(step):
+        chunk = chunk_of(step)
         cols = pl.ds(pl.multiple_of(chunk * width, width), width)
         cb = cos_b[:, cols]
         sb = sin_b[:, cols]
@@ -330,10 +383,9 @@
 
         parts = []
         sums = []
+        both = jnp.dot(snaps[...], table[...], preferred_element_type=f32).astype(jnp.bfloat16)
         for snap in range(snap_count):
-            spectra = jnp.dot(snaps[snap], table[...], preferred_element_type=f32).astype(
-                jnp.bfloat16
-            )
+            spectra = both[snap * channels : (snap + 1) * channels]
             wide = spectra.astype(f32)
             sums.append(jnp.broadcast_to(jnp.sum(wide * wide, axis=0, keepdims=True), (8, width)))
             parts.append(jnp.dot(shapes, spectra, preferred_element_type=f32))
@@ -341,35 +393,62 @@
             lanes = slice(pair * LANES, (pair + 1) * LANES)
             p0, p1 = parts[0][:, lanes], parts[1][:, lanes]
             t0, t1 = sums[0][:, lanes], sums[1][:, lanes]
-            for side in range(2):
-                dest = chunk * per_chunk + 2 * pair + side
-                if side == 0:
-                    message = jnp.where(wide_low, p0, pltpu.roll(p1, LANES // 2, 1))
-                    trace = jnp.where(thin_low, t0, pltpu.roll(t1, LANES // 2, 1))
-                else:
-                    message = jnp.where(wide_low, pltpu.roll(p0, LANES // 2, 1), p1)
-                    trace = jnp.where(thin_low, pltpu.roll(t0, LANES // 2, 1), t1)
-                proj_send[dest] = message.astype(jnp.bfloat16)
-                trace_send[dest] = trace
-
-                @pl.when(dest != me)
-                def _():
-                    send(
-                        proj_send.at[dest],
-                        proj_recv.at[me],
-                        proj_ssem.at[dest],
-                        proj_rsem.at[me],
-                        dest,
-                    ).start()
-                    send(
-                        trace_send.at[dest],
-                        trace_recv.at[me],
-                        trace_ssem.at[dest],
-                        trace_rsem.at[me],
-                        dest,
-                    ).start()
-
-    proj_recv[me] = proj_send[me]
+            first = jnp.where(wide_low, p0, pltpu.roll(p1, LANES // 2, 1))
+            second = jnp.where(wide_low, pltpu.roll(p0, LANES // 2, 1), p1)
+            kept[chunk, pair] = jnp.where(core == 0, first, second)
+            core_send[chunk, pair] = jnp.where(core == 0, second, first).astype(jnp.bfloat16)
+            dest = chunk * per_chunk + 2 * pair
+            trace_send[dest] = jnp.where(thin_low, t0, pltpu.roll(t1, LANES // 2, 1))[:1]
+            trace_send[dest + 1] = jnp.where(thin_low, pltpu.roll(t0, LANES // 2, 1), t1)[:1]
+        core_copy(chunk).start()
+        for k in range(per_chunk):
+            dest = chunk * per_chunk + k
+
+            @pl.when(dest != me)
+            def _():
+                send(
+                    trace_send.at[dest],
+                    trace_recv.at[me],
+                    trace_ssem.at[dest],
+                    trace_rsem.at[me],
+                    dest,
+                ).start()
+
+    def add_core(step):
+        chunk = chunk_of(step)
+        core_copy(chunk).wait_recv()
+        side_kept[chunk] = kept[chunk, side] + core_recv[chunk, side].astype(f32)
+        side_send[chunk] = (kept[chunk, 1 - side] + core_recv[chunk, 1 - side].astype(f32)).astype(
+            jnp.bfloat16
+        )
+        side_copy(chunk).start()
+
+    def add_side(step, keep=False):
+        chunk = chunk_of(step)
+        side_copy(chunk).wait_recv()
+        total = side_kept[chunk] + side_recv[chunk].astype(f32)
+        if keep:
+            far_kept[...] = total
+        else:
+            far_send[chunk] = total.astype(jnp.bfloat16)
+            far_copy(chunk, far).start()
+
+    last = chunk_count - 1
+
+    @pl.loop(0, chunk_count)
+    def _(step):
+        make(step)
+
+        @pl.when(step >= 1)
+        def _():
+            add_core(step - 1)
+
+        @pl.when(step >= 2)
+        def _():
+            add_side(step - 2)
+
+    add_core(last)
+    add_side(last - 1)
     trace_recv[me] = trace_send[me]
 
     @pl.loop(1, devices)
@@ -384,17 +463,28 @@
         ).wait_recv()
 
     gram = gram_full[...].astype(jnp.bfloat16).astype(f32)
+    wide_lane = lax.broadcasted_iota(jnp.int32, (modes, LANES), 1)
+    mode_ids = lax.broadcasted_iota(jnp.int32, (modes, depths), 0)
+    sources = []
     waves_sin = []
     waves_cos = []
     norms = []
     for block in range(blocks):
-        phases = phases_ref[block]
+        wave = waves_ref[owners[block], :, pl.ds(pl.multiple_of((me // 4) * LANES, LANES), LANES)]
+        wave = jnp.where(wide_lane // quarter == me % 4, wave, 0.0)
+        wave = wave + pltpu.roll(wave, quarter, 1)
+        wave = wave + pltpu.roll(wave, 2 * quarter, 1)
+        range_ids = block * RPB + wide_lane // quarter
+        phases = wave * (range_start + range_step * range_ids.astype(f32))
         sine, cosine = sincos_wide(phases)
         scale = 1.0 / jnp.sqrt(phases)
         sine, cosine = sine * scale, cosine * scale
         waves_sin.append(sine)
         waves_cos.append(cosine)
-        source = source_ref[block]
+        source = jnp.where(
+            mode_ids < counts_ref[owners[block]], modes_source_ref[owners[block]], 0.0
+        )
+        sources.append(source)
         rows = slice((block // 2) * modes, (block // 2 + 1) * modes)
         for m in range(modes):
             lane = (block % 2) * modes + m
@@ -414,12 +504,11 @@
             )
         )
 
+    add_side(last, keep=True)
+
     @pl.loop(1, devices)
     def _(step):
         peer = (me + step) % devices
-        send(
-            proj_send.at[peer], proj_recv.at[peer], proj_ssem.at[peer], proj_rsem.at[peer], peer
-        ).wait_recv()
         send(
             trace_send.at[peer],
             trace_recv.at[peer],
@@ -428,12 +517,13 @@
             peer,
         ).wait_recv()
 
-    proj = proj_recv[0].astype(f32)
-    for source_id in range(1, devices):
-        proj = proj + proj_recv[source_id].astype(f32)
+    proj = far_kept[...]
+    for step in range(1, chunk_count):
+        slot = (far + step) % chunk_count
+        far_copy(slot, slot).wait_recv()
+        proj = proj + far_recv[slot].astype(f32)
     proj = proj.astype(jnp.bfloat16)
-    trace = jnp.sum(trace_recv[...], axis=0)
-    quarter = LANES // 4
+    trace = jnp.broadcast_to(jnp.sum(trace_recv[...], axis=0), (8, LANES))
     trace = trace + pltpu.roll(trace, 2 * quarter, 1)
     trace = trace + pltpu.roll(trace, quarter, 1)
     level = (1.0 / jnp.sqrt(snap_count * trace))[:1]
@@ -454,7 +544,7 @@
         coupled = jnp.concatenate(coupled, axis=1)
         coupled_high = coupled.astype(jnp.bfloat16)
         coupled_low = (coupled - coupled_high.astype(f32)).astype(jnp.bfloat16)
-        source = source_ref[block]
+        source = sources[block]
         source_high = source.astype(jnp.bfloat16)
         source_low = (source - source_high.astype(f32)).astype(jnp.bfloat16)
         beams = lax.dot_general(
@@ -506,12 +596,18 @@
             gram_own, gram_full.at[own_rows, :], full_ssem.at[peer], full_rsem.at[me], peer
         ).wait_send()
         send(
-            proj_send.at[peer], proj_recv.at[me], proj_ssem.at[peer], proj_rsem.at[me], peer
-        ).wait_send()
-        send(
             trace_send.at[peer], trace_recv.at[me], trace_ssem.at[peer], trace_rsem.at[me], peer
         ).wait_send()
         send(surf_own, surf_recv.at[me], surf_ssem.at[peer], surf_rsem.at[me], peer).wait_send()
+
+    @pl.loop(0, chunk_count)
+    def _(chunk):
+        core_copy(chunk).wait_send()
+        side_copy(chunk).wait_send()
+
+        @pl.when(chunk != far)
+        def _():
+            far_copy(chunk, far).wait_send()
 
 
 def per_device_fused(
@@ -522,41 +618,38 @@
     segs, modes, depths = source_modes.shape
     blocks = segment_owner.shape[0]
     freqs = freq_bins.shape[0]
-    local_freqs = freqs // devices
     columns = 2 * freqs
     half = math.isqrt(samples)
-    freq_columns = jnp.broadcast_to(
-        freq_bins.reshape(devices, 1, local_freqs), (devices, 2, local_freqs)
-    ).reshape(1, columns)
-    shapes = jnp.take(mode_shapes, segment_owner, axis=0).reshape(blocks * modes, channels)
-    active = jnp.arange(modes, dtype=jnp.int32)[None, :] < mode_counts[:, None]
-    masked = jnp.take(source_modes * active[:, :, None], segment_owner, axis=0)
-    first_freq = lax.axis_index("chan") * local_freqs
-    waves = lax.dynamic_slice_in_dim(wavenumbers, first_freq, local_freqs, 2)
-    waves = jnp.take(waves, segment_owner, axis=0)
-    ranges = range_start + range_step * jnp.arange(blocks * RPB, dtype=jnp.float32)
-    phases = waves[:, :, None, :] * ranges.reshape(blocks, 1, RPB, 1)
-    phases = phases.reshape(blocks, modes, RPB * local_freqs)
+    rows = blocks * modes
     f32, bf16 = jnp.float32, jnp.bfloat16
     ranges_total = blocks * RPB
     dma = pltpu.SemaphoreType.DMA((devices,))
     vmem = pl.BlockSpec(memory_space=pltpu.VMEM)
+    smem = pl.BlockSpec(memory_space=pltpu.SMEM)
+    few = pltpu.SemaphoreType.DMA((devices // 4,))
     return pl.pallas_call(
         functools.partial(fused_kernel, devices),
         out_shape=jax.ShapeDtypeStruct((1, depths), f32),
-        in_specs=[vmem, pl.BlockSpec(memory_space=pl.ANY), vmem, vmem, vmem],
+        in_specs=[vmem, pl.BlockSpec(memory_space=pl.ANY), vmem, smem, vmem, vmem, smem],
         out_specs=vmem,
         scratch_shapes=[
-            pltpu.VMEM((snap_count, channels, samples), bf16),
+            pltpu.VMEM((snap_count * channels, samples), bf16),
             pltpu.VMEM((samples, 256), bf16),
             pltpu.VMEM((half, columns), f32),
             pltpu.VMEM((half, columns), f32),
             pltpu.VMEM((half, columns), f32),
             pltpu.VMEM((half, columns), f32),
-            pltpu.VMEM((devices, blocks * modes, LANES), bf16),
-            pltpu.VMEM((devices, blocks * modes, LANES), bf16),
-            pltpu.VMEM((devices, 8, LANES), f32),
-            pltpu.VMEM((devices, 8, LANES), f32),
+            pltpu.VMEM((devices // 4, 2, rows, LANES), f32),
+            pltpu.VMEM((devices // 4, 2, rows, LANES), bf16),
+            pltpu.VMEM((devices // 4, 2, rows, LANES), bf16),
+            pltpu.VMEM((devices // 4, rows, LANES), f32),
+            pltpu.VMEM((devices // 4, rows, LANES), bf16),
+            pltpu.VMEM((devices // 4, rows, LANES), bf16),
+            pltpu.VMEM((rows, LANES), f32),
+            pltpu.VMEM((devices // 4, rows, LANES), bf16),
+            pltpu.VMEM((devices // 4, rows, LANES), bf16),
+            pltpu.VMEM((devices, 1, LANES), f32),
+            pltpu.VMEM((devices, 1, LANES), f32),
             pltpu.VMEM((devices * 8, LANES), f32),
             pltpu.VMEM((devices, 8, LANES), f32),
             pltpu.VMEM((8, LANES), f32),
@@ -568,11 +661,20 @@
             pltpu.VMEM((ranges_total, depths), f32),
             pltpu.SemaphoreType.DMA,
         ]
-        + [dma] * 10,
+        + [few] * 6
+        + [dma] * 8,
         compiler_params=pltpu.CompilerParams(
             collective_id=0, has_side_effects=True, vmem_limit_bytes=40 * 2**20
         ),
-    )(freq_columns, snapshots, shapes, phases, masked)
+    )(
+        freq_bins.reshape(freqs // LANES, LANES),
+        snapshots.reshape(snap_count * channels, samples),
+        mode_shapes,
+        mode_counts,
+        wavenumbers,
+        source_modes,
+        segment_owner,
+    )
 
 
 def per_device(*args):

time: 58.4 us -> 45.1 us (0.77)
  Pallas kernels: 46.5 us -> 37 us
  other arithmetic: 3.42 us -> 0 us
    pallas_call x1, Pallas kernels: 46.5 us -> 37 us  [per_device_fused(): pl.pallas_call(functools.partial(fused_kernel, devices), out_shape=jax.Sh...]
    unnamed x5 -> x15, local copies, waits for them, and re-layouts: 3.93 us -> 7.81 us
    gather x3 -> x0, local copies, waits for them, and re-layouts: 2.62 us -> none  [the longest x1 1.51 us: per_device_fused(): jnp.take(mode_shapes, segment_owner, axis=0)]
    mul x1 -> x0, other arithmetic: 1.08 us -> none  [per_device_fused(): masked = jnp.take(source_modes * active[:, :, None], segment_owner, axis=0)]
    select_n x4 -> x0, other arithmetic: 0.93 us -> none  [the longest x2 0.76 us: per_device_fused(): jnp.take(mode_shapes, segment_owner, axis=0)]
    broadcast_in_dim x4 -> x0, local copies, waits for them, and re-layouts: 0.93 us -> none  [the longest x2 0.77 us: per_device_fused(): jnp.broadcast_to(freq_bins.reshape(devices, 1, local_freqs), (devices, 2,...]
    convert_element_type x1 -> x0, other arithmetic: 0.73 us -> none  [per_device_fused(): masked = jnp.take(source_modes * active[:, :, None], segment_owner, axis=0)]
    and x1 -> x0, other arithmetic: 0.66 us -> none  [per_device_fused(): jnp.take(mode_shapes, segment_owner, axis=0)]
where the time goes in v2:
time: 45.1 us; the launch traced here: 44.8 us
  Pallas kernels  37 us (82%)
  local copies, waits for them, and re-layouts  7.81 us (17%)
    pallas_call x1, Pallas kernels, per_device_fused(): pl.pallas_call(functools.partial(fused_kernel, devices), out_shape=jax.Sh...  37 us
    unnamed x15, local copies, waits for them, and re-layouts  7.81 us

profile of v2, /device:TPU:0, one launch (start us, length us, event | category | flops | bytes accessed | tf_op | source)
XLA Modules:
  0.0 44.8 jit_solution(8358528144205198023)
XLA Ops:
  0.0 0.0 copy-start
  0.0 2.2 %copy-done = bf16[2,256,4096]{2,1,0:T(8,128)(2,1)S(1)} copy-done((bf16[2,256,4096]{2,1,0:T(8,128)(2,1)S(1)}, bf16[2,256,4096]{2,1,0:T(8,128)(2,1)}, u32[]{:S(2)}) %copy-start) | copy-done | bytes 4194328
  2.2 0.0 copy-start.1
  2.2 1.2 %copy-done.1 = f32[8,64,512]{2,1,0:T(8,128)S(1)} copy-done((f32[8,64,512]{2,1,0:T(8,128)S(1)}, f32[8,64,512]{2,1,0:T(8,128)}, u32[]{:S(2)}) %copy-start.1) | copy-done | bytes 1048600
  3.4 0.0 copy-start.2
  3.4 0.9 %copy-done.2 = bf16[8,64,256]{2,1,0:T(8,128)(2,1)S(1)} copy-done((bf16[8,64,256]{2,1,0:T(8,128)(2,1)S(1)}, bf16[8,64,256]{2,1,0:T(8,128)(2,1)}, u32[]{:S(2)}) %copy-start.2) | copy-done | bytes 262168
  4.4 0.0 copy-start.3
  4.4 0.9 %copy-done.3 = f32[8,64,128]{2,1,0:T(8,128)S(1)} copy-done((f32[8,64,128]{2,1,0:T(8,128)S(1)}, f32[8,64,128]{2,1,0:T(8,128)}, u32[]{:S(2)}) %copy-start.3) | copy-done | bytes 262168
  5.3 0.0 copy-start.4
  5.3 0.7 %copy-done.4 = s32[512]{0:T(512)S(1)} copy-done((s32[512]{0:T(512)S(1)}, s32[512]{0:T(512)}, u32[]{:S(2)}) %copy-start.4) | copy-done | bytes 2072
  6.0 0.0 copy-start.5
  6.0 0.7 %copy-done.5 = s32[8]{0:T(128)S(1)} copy-done((s32[8]{0:T(128)S(1)}, s32[8]{0:T(128)}, u32[]{:S(2)}) %copy-start.5) | copy-done | bytes 56
  6.7 0.0 copy-start.6
  6.7 0.7 %copy-done.6 = s32[4]{0:T(128)S(1)} copy-done((s32[4]{0:T(128)S(1)}, s32[4]{0:T(128)}, u32[]{:S(2)}) %copy-start.6) | copy-done | bytes 40
  7.3 37.0 %shard_map.73 = f32[1,128]{1,0:T(1,128)S(1)} custom-call(s32[4,128]{1,0:T(4,128)S(1)} %bitcast.3, bf16[512,4096]{1,0:T(8,128)(2,1)S(1)} %bitcast.2, bf16[8,64,256]{2,1,0:T(8,128)(2,1)S(1)} %copy-done.2, s32[8]{0:T(128)S(1)} %copy-done.5, f32[8,64,512]{2,1,0:T(8,128)S(1)} %copy-done.1, f32[8,64,128]{2,1,0:T(8,128)S(1)} %copy-done.3, s32[4]{0:T(128)S(1)} %copy-done.6), custom_call_target="tpu_custom_call" | custom-call | tf_op jit(solution)/shard_map/pallas_call | solution.py:630
  44.3 0.5 %copy.9 = f32[1,128]{1,0:T(1,128)} copy(f32[1,128]{1,0:T(1,128)S(1)} %shard_map.73) | data formatting | bytes 1024
Async XLA Ops:
  0.0 2.2 %copy-start = (bf16[2,256,4096]{2,1,0:T(8,128)(2,1)S(1)}, bf16[2,256,4096]{2,1,0:T(8,128)(2,1)}, u32[]{:S(2)}) copy-start(bf16[2,256,4096]{2,1,0:T(8,128)(2,1)} %param.7) | copy-start | bytes 12582916
  2.2 1.2 %copy-start.1 = (f32[8,64,512]{2,1,0:T(8,128)S(1)}, f32[8,64,512]{2,1,0:T(8,128)}, u32[]{:S(2)}) copy-start(f32[8,64,512]{2,1,0:T(8,128)} %waves_ref.1) | copy-start | bytes 3145732
  3.4 0.9 %copy-start.2 = (bf16[8,64,256]{2,1,0:T(8,128)(2,1)S(1)}, bf16[8,64,256]{2,1,0:T(8,128)(2,1)}, u32[]{:S(2)}) copy-start(bf16[8,64,256]{2,1,0:T(8,128)(2,1)} %modes_ref.1) | copy-start | bytes 786436
  4.4 0.9 %copy-start.3 = (f32[8,64,128]{2,1,0:T(8,128)S(1)}, f32[8,64,128]{2,1,0:T(8,128)}, u32[]{:S(2)}) copy-start(f32[8,64,128]{2,1,0:T(8,128)} %modes_source_ref.1) | copy-start | bytes 786436
  5.3 0.7 %copy-start.4 = (s32[512]{0:T(512)S(1)}, s32[512]{0:T(512)}, u32[]{:S(2)}) copy-start(s32[512]{0:T(512)} %param.8) | copy-start | bytes 6148
  6.0 0.7 %copy-start.5 = (s32[8]{0:T(128)S(1)}, s32[8]{0:T(128)}, u32[]{:S(2)}) copy-start(s32[8]{0:T(128)} %counts_ref.1) | copy-start | bytes 100
  6.7 0.7 %copy-start.6 = (s32[4]{0:T(128)S(1)}, s32[4]{0:T(128)}, u32[]{:S(2)}) copy-start(s32[4]{0:T(128)} %owner_ref.1) | copy-start | bytes 52

commit v3 on v2

--- a/solution.py
+++ b/solution.py
@@ -185,14 +185,20 @@
 
 def fused_kernel(
     devices,
+    freq_hbm,
+    snaps_hbm,
+    modes_hbm,
+    counts_hbm,
+    waves_hbm,
+    source_hbm,
+    owner_hbm,
+    out_ref,
     freq_ref,
-    snaps_hbm,
     modes_ref,
     counts_ref,
     waves_ref,
     modes_source_ref,
     owner_ref,
-    out_ref,
     snaps,
     table,
     cos_a,
@@ -255,8 +261,23 @@
         pl.semaphore_signal(
             barrier, inc=1, device_id={"chan": (me + step) % devices}, device_id_type=MESH
         )
-    load = pltpu.make_async_copy(snaps_hbm, snaps, load_sem)
-    load.start()
+    window = pl.ds(pl.multiple_of((me // 4) * LANES, LANES), LANES)
+    loads = [
+        pltpu.make_async_copy(src, dst, load_sem.at[n])
+        for n, (src, dst) in enumerate(
+            [
+                (freq_hbm, freq_ref),
+                (owner_hbm, owner_ref),
+                (counts_hbm, counts_ref),
+                (modes_hbm, modes_ref),
+                (source_hbm, modes_source_ref),
+                (waves_hbm.at[:, :, window], waves_ref),
+                (snaps_hbm, snaps),
+            ]
+        )
+    ]
+    for load in loads:
+        load.start()
 
     def send(src, dst, ssem, rsem, peer):
         return pltpu.make_async_remote_copy(
@@ -268,33 +289,8 @@
             device_id_type=MESH,
         )
 
-    owners = [owner_ref[block] for block in range(blocks)]
-    shapes = jnp.concatenate([modes_ref[owner] for owner in owners], axis=0)
-    inner = lax.dot_general(shapes, shapes, (((1,), (1,)), ((), ())), preferred_element_type=f32)
-    low_half = lax.broadcasted_iota(jnp.int32, (modes, LANES), 1) < modes
-    for pair in range(blocks // 2):
-        base = pair * LANES
-        gram_part[pair * modes : (pair + 1) * modes, :] = jnp.where(
-            low_half,
-            inner[base : base + modes, base : base + LANES],
-            inner[base + modes : base + LANES, base : base + LANES],
-        )
-    pl.semaphore_wait(barrier, devices - 1)
-
-    @pl.loop(1, devices)
-    def _(step):
-        peer = (me + step) % devices
-        send(
-            gram_part.at[pl.ds(pl.multiple_of(peer * 8, 8), 8), :],
-            gram_recv.at[me],
-            gram_ssem.at[peer],
-            gram_rsem.at[me],
-            peer,
-        ).start()
-
-    gram_recv[me] = gram_part[pl.ds(pl.multiple_of(me * 8, 8), 8), :]
-
     half = cos_a.shape[0]
+    loads[0].wait()
     lane = lax.broadcasted_iota(jnp.int32, (1, LANES), 1)
     quarter = LANES // 4
     group = lane // quarter
@@ -322,29 +318,37 @@
     sin_b[...] = sin_v
     cos_b[...] = cos_v
 
+    for load in loads[1:4]:
+        load.wait()
+    owners = [owner_ref[block] for block in range(blocks)]
+    shapes = jnp.concatenate([modes_ref[owner] for owner in owners], axis=0)
+    inner = lax.dot_general(shapes, shapes, (((1,), (1,)), ((), ())), preferred_element_type=f32)
+    low_half = lax.broadcasted_iota(jnp.int32, (modes, LANES), 1) < modes
+    for pair in range(blocks // 2):
+        base = pair * LANES
+        gram_part[pair * modes : (pair + 1) * modes, :] = jnp.where(
+            low_half,
+            inner[base : base + modes, base : base + LANES],
+            inner[base + modes : base + LANES, base : base + LANES],
+        )
+    pl.semaphore_wait(barrier, devices - 1)
+
     @pl.loop(1, devices)
     def _(step):
         peer = (me + step) % devices
         send(
-            gram_part.at[pl.ds(0, 8), :],
-            gram_recv.at[peer],
+            gram_part.at[pl.ds(pl.multiple_of(peer * 8, 8), 8), :],
+            gram_recv.at[me],
             gram_ssem.at[peer],
-            gram_rsem.at[peer],
+            gram_rsem.at[me],
             peer,
-        ).wait_recv()
-
-    gram_own[...] = jnp.sum(gram_recv[...], axis=0)
+        ).start()
+
+    gram_recv[me] = gram_part[pl.ds(pl.multiple_of(me * 8, 8), 8), :]
+
+    for load in loads[4:]:
+        load.wait()
     own_rows = pl.ds(pl.multiple_of(me * 8, 8), 8)
-    gram_full[own_rows, :] = gram_own[...]
-
-    @pl.loop(1, devices)
-    def _(step):
-        peer = (me + step) % devices
-        send(
-            gram_own, gram_full.at[own_rows, :], full_ssem.at[peer], full_rsem.at[me], peer
-        ).start()
-
-    load.wait()
     per_chunk = width // (columns // devices)
     chunk_count = columns // width
     wide_low = lax.broadcasted_iota(jnp.int32, (blocks * modes, LANES), 1) < LANES // 2
@@ -373,17 +377,23 @@
         cb = cos_b[:, cols]
         sb = sin_b[:, cols]
 
-        @pl.loop(0, half, unroll=4)
-        def _(a):
-            ca = cos_a[pl.ds(a, 1), cols]
-            sa = sin_a[pl.ds(a, 1), cols]
-            table[pl.ds(pl.multiple_of(a * half, half), half), :] = (ca * cb - sa * sb).astype(
-                jnp.bfloat16
-            )
+        def build(first):
+            for a in range(first, first + half // 4):
+                ca = cos_a[a : a + 1, cols]
+                sa = sin_a[a : a + 1, cols]
+                table[a * half : (a + 1) * half, :] = (ca * cb - sa * sb).astype(jnp.bfloat16)
 
         parts = []
         sums = []
-        both = jnp.dot(snaps[...], table[...], preferred_element_type=f32).astype(jnp.bfloat16)
+        build(0)
+        both = None
+        for quart in range(4):
+            rows = slice(quart * samples // 4, (quart + 1) * samples // 4)
+            term = jnp.dot(snaps[:, rows], table[rows, :], preferred_element_type=f32)
+            if quart < 3:
+                build((quart + 1) * half // 4)
+            both = term if both is None else both + term
+        both = both.astype(jnp.bfloat16)
         for snap in range(snap_count):
             spectra = both[snap * channels : (snap + 1) * channels]
             wide = spectra.astype(f32)
@@ -433,11 +443,37 @@
             far_send[chunk] = total.astype(jnp.bfloat16)
             far_copy(chunk, far).start()
 
+    def gram_share():
+        @pl.loop(1, devices)
+        def _(step):
+            peer = (me + step) % devices
+            send(
+                gram_part.at[pl.ds(0, 8), :],
+                gram_recv.at[peer],
+                gram_ssem.at[peer],
+                gram_rsem.at[peer],
+                peer,
+            ).wait_recv()
+
+        gram_own[...] = jnp.sum(gram_recv[...], axis=0)
+        gram_full[own_rows, :] = gram_own[...]
+
+        @pl.loop(1, devices)
+        def _(step):
+            peer = (me + step) % devices
+            send(
+                gram_own, gram_full.at[own_rows, :], full_ssem.at[peer], full_rsem.at[me], peer
+            ).start()
+
     last = chunk_count - 1
 
     @pl.loop(0, chunk_count)
     def _(step):
         make(step)
+
+        @pl.when(step == 0)
+        def _():
+            gram_share()
 
         @pl.when(step >= 1)
         def _():
@@ -470,7 +506,7 @@
     waves_cos = []
     norms = []
     for block in range(blocks):
-        wave = waves_ref[owners[block], :, pl.ds(pl.multiple_of((me // 4) * LANES, LANES), LANES)]
+        wave = waves_ref[owners[block]]
         wave = jnp.where(wide_lane // quarter == me % 4, wave, 0.0)
         wave = wave + pltpu.roll(wave, quarter, 1)
         wave = wave + pltpu.roll(wave, 2 * quarter, 1)
@@ -625,14 +661,19 @@
     ranges_total = blocks * RPB
     dma = pltpu.SemaphoreType.DMA((devices,))
     vmem = pl.BlockSpec(memory_space=pltpu.VMEM)
-    smem = pl.BlockSpec(memory_space=pltpu.SMEM)
     few = pltpu.SemaphoreType.DMA((devices // 4,))
     return pl.pallas_call(
         functools.partial(fused_kernel, devices),
         out_shape=jax.ShapeDtypeStruct((1, depths), f32),
-        in_specs=[vmem, pl.BlockSpec(memory_space=pl.ANY), vmem, smem, vmem, vmem, smem],
+        in_specs=[pl.BlockSpec(memory_space=pltpu.HBM)] * 7,
         out_specs=vmem,
         scratch_shapes=[
+            pltpu.VMEM((freqs // LANES, LANES), jnp.int32),
+            pltpu.VMEM((segs, modes, channels), bf16),
+            pltpu.SMEM((segs,), jnp.int32),
+            pltpu.VMEM((segs, modes, LANES), f32),
+            pltpu.VMEM((segs, modes, depths), f32),
+            pltpu.SMEM((blocks,), jnp.int32),
             pltpu.VMEM((snap_count * channels, samples), bf16),
             pltpu.VMEM((samples, 256), bf16),
             pltpu.VMEM((half, columns), f32),
@@ -659,12 +700,12 @@
             pltpu.VMEM((ranges_total, depths), f32),
             pltpu.VMEM((devices, ranges_total, depths), f32),
             pltpu.VMEM((ranges_total, depths), f32),
-            pltpu.SemaphoreType.DMA,
+            pltpu.SemaphoreType.DMA((7,)),
         ]
         + [few] * 6
         + [dma] * 8,
         compiler_params=pltpu.CompilerParams(
-            collective_id=0, has_side_effects=True, vmem_limit_bytes=40 * 2**20
+            collective_id=0, has_side_effects=True, vmem_limit_bytes=62 * 2**20
         ),
     )(
         freq_bins.reshape(freqs // LANES, LANES),

time: 45.1 us -> 34.9 us (0.77)
  local copies, waits for them, and re-layouts: 7.81 us -> 1.19 us
  Pallas kernels: 37 us -> 33.5 us
    unnamed x15 -> x1, local copies, waits for them, and re-layouts: 7.81 us -> 1.19 us
    pallas_call x1, Pallas kernels: 37 us -> 33.5 us  [per_device_fused(): pl.pallas_call(functools.partial(fused_kernel, devices), out_shape=jax.Sh...]
where the time goes in v3:
time: 34.9 us; the launch traced here: 34.7 us
  Pallas kernels  33.5 us (96%)
  local copies, waits for them, and re-layouts  1.19 us (3%)
    pallas_call x1, Pallas kernels, per_device_fused(): pl.pallas_call(functools.partial(fused_kernel, devices), out_shape=jax.Sh...  33.5 us
    unnamed x1, local copies, waits for them, and re-layouts  1.19 us

profile of v3, /device:TPU:0, one launch (start us, length us, event | category | flops | bytes accessed | tf_op | source)
XLA Modules:
  0.0 34.7 jit_solution(13118258981515148420)
XLA Ops:
  0.0 33.5 %shard_map.73 = f32[1,128]{1,0:T(1,128)} custom-call(s32[4,128]{1,0:T(4,128)} %bitcast.3, bf16[512,4096]{1,0:T(8,128)(2,1)} %bitcast.2, bf16[8,64,256]{2,1,0:T(8,128)(2,1)} %modes_hbm.1, s32[8]{0:T(128)} %counts_hbm.1, f32[8,64,512]{2,1,0:T(8,128)} %waves_hbm.1, f32[8,64,128]{2,1,0:T(8,128)} %source_hbm.1, s32[4]{0:T(128)} %owner_hbm.1), custom_call_target="tpu_custom_call" | custom-call | tf_op jit(solution)/shard_map/pallas_call | solution.py:665
  33.5 1.2 %copy.9 = f32[1,128]{1,0:T(1,128)} copy(f32[1,128]{1,0:T(1,128)} %shard_map.73) | data formatting | bytes 1024

commit v4 on v3

--- a/solution.py
+++ b/solution.py
@@ -499,6 +499,11 @@
         ).wait_recv()
 
     gram = gram_full[...].astype(jnp.bfloat16).astype(f32)
+    tile = 16
+    first_tile = (lax.broadcasted_iota(jnp.int32, gram.shape, 0) % modes) // tile
+    second_tile = (lax.broadcasted_iota(jnp.int32, gram.shape, 1) % modes) // tile
+    gram = jnp.where(first_tile > second_tile, 2.0 * gram, gram)
+    pairs = sum(tile * (modes - start) for start in range(0, modes, tile))
     wide_lane = lax.broadcasted_iota(jnp.int32, (modes, LANES), 1)
     mode_ids = lax.broadcasted_iota(jnp.int32, (modes, depths), 0)
     sources = []
@@ -521,20 +526,23 @@
             mode_ids < counts_ref[owners[block]], modes_source_ref[owners[block]], 0.0
         )
         sources.append(source)
-        rows = slice((block // 2) * modes, (block // 2 + 1) * modes)
+        base = (block // 2) * modes
+        filled = 0
         for m in range(modes):
+            low = m // tile * tile
             lane = (block % 2) * modes + m
-            at = slice(m * modes, (m + 1) * modes)
-            terms_a[at, :] = (cosine[m : m + 1] * cosine + sine[m : m + 1] * sine).astype(
-                jnp.bfloat16
-            )
+            at = slice(filled, filled + modes - low)
+            filled += modes - low
+            terms_a[at, :] = (
+                cosine[m : m + 1] * cosine[low:] + sine[m : m + 1] * sine[low:]
+            ).astype(jnp.bfloat16)
             terms_b[at, :] = (
-                gram[rows, lane : lane + 1] * (source[m : m + 1] * source)
+                gram[base + low : base + modes, lane : lane + 1] * (source[m : m + 1] * source[low:])
             ).astype(jnp.bfloat16)
         norms.append(
             lax.dot_general(
-                terms_a[...],
-                terms_b[...],
+                terms_a[:pairs],
+                terms_b[:pairs],
                 (((0,), (0,)), ((), ())),
                 preferred_element_type=f32,
             )
@@ -602,19 +610,39 @@
                 ratio[j * quarter : (j + 1) * quarter], axis=0, keepdims=True
             )
 
-    surf_recv[me] = surf_own[...]
-
-    @pl.loop(1, devices)
-    def _(step):
-        peer = (me + step) % devices
-        send(surf_own, surf_recv.at[me], surf_ssem.at[peer], surf_rsem.at[me], peer).start()
-
-    @pl.loop(1, devices)
-    def _(step):
-        peer = (me + step) % devices
-        send(surf_own, surf_recv.at[peer], surf_ssem.at[peer], surf_rsem.at[peer], peer).wait_recv()
-
-    total = jnp.sum(surf_recv[...], axis=0) / (columns // 2)
+    near = me % 4
+
+    def near_copy(step, slot):
+        peer = (near + step) % 4
+        return send(
+            surf_own, surf_recv.at[slot], surf_ssem.at[peer], surf_rsem.at[slot], far * 4 + peer
+        )
+
+    def wide_copy(step, slot):
+        peer = (far + step) % chunk_count
+        return send(
+            surf_recv.at[4 + far],
+            surf_recv.at[4 + slot],
+            surf_ssem.at[4 + peer],
+            surf_rsem.at[4 + slot],
+            peer * 4 + near,
+        )
+
+    for step in range(1, 4):
+        near_copy(step, near).start()
+    mid = surf_own[...]
+    for step in range(1, 4):
+        near_copy(step, (near + step) % 4).wait_recv()
+        mid = mid + surf_recv[(near + step) % 4]
+    surf_recv[4 + far] = mid
+    for step in range(1, chunk_count):
+        wide_copy(step, far).start()
+    for step in range(1, chunk_count):
+        wide_copy(step, (far + step) % chunk_count).wait_recv()
+    total = surf_recv[4]
+    for step in range(1, chunk_count):
+        total = total + surf_recv[4 + step]
+    total = total / (columns // 2)
     total_ref[...] = total
     out_ref[...] = total_ref[pl.ds(me, 1), :] / jnp.max(total)
 
@@ -634,7 +662,11 @@
         send(
             trace_send.at[peer], trace_recv.at[me], trace_ssem.at[peer], trace_rsem.at[me], peer
         ).wait_send()
-        send(surf_own, surf_recv.at[me], surf_ssem.at[peer], surf_rsem.at[me], peer).wait_send()
+
+    for step in range(1, 4):
+        near_copy(step, near).wait_send()
+    for step in range(1, chunk_count):
+        wide_copy(step, far).wait_send()
 
     @pl.loop(0, chunk_count)
     def _(chunk):
@@ -698,7 +730,7 @@
             pltpu.VMEM((modes * modes, LANES), bf16),
             pltpu.VMEM((modes * modes, LANES), bf16),
             pltpu.VMEM((ranges_total, depths), f32),
-            pltpu.VMEM((devices, ranges_total, depths), f32),
+            pltpu.VMEM((4 + devices // 4, ranges_total, depths), f32),
             pltpu.VMEM((ranges_total, depths), f32),
             pltpu.SemaphoreType.DMA((7,)),
         ]

time: 34.9 us -> 36.2 us (1.037)
  Pallas kernels: 33.5 us -> 34.9 us
    pallas_call x1, Pallas kernels: 33.5 us -> 34.9 us  [per_device_fused(): pl.pallas_call(functools.partial(fused_kernel, devices), out_shape=jax.Sh...]
where the time goes in v4:
time: 36.2 us; the launch traced here: 36.1 us
  Pallas kernels  34.9 us (96%)
  local copies, waits for them, and re-layouts  1.19 us (3%)
    pallas_call x1, Pallas kernels, per_device_fused(): pl.pallas_call(functools.partial(fused_kernel, devices), out_shape=jax.Sh...  34.9 us
    unnamed x1, local copies, waits for them, and re-layouts  1.19 us

profile of v4, /device:TPU:0, one launch (start us, length us, event | category | flops | bytes accessed | tf_op | source)
XLA Modules:
  0.0 36.1 jit_solution(6338735667276916282)
XLA Ops:
  0.0 34.9 %shard_map.73 = f32[1,128]{1,0:T(1,128)} custom-call(s32[4,128]{1,0:T(4,128)} %bitcast.3, bf16[512,4096]{1,0:T(8,128)(2,1)} %bitcast.2, bf16[8,64,256]{2,1,0:T(8,128)(2,1)} %modes_hbm.1, s32[8]{0:T(128)} %counts_hbm.1, f32[8,64,512]{2,1,0:T(8,128)} %waves_hbm.1, f32[8,64,128]{2,1,0:T(8,128)} %source_hbm.1, s32[4]{0:T(128)} %owner_hbm.1), custom_call_target="tpu_custom_call" | custom-call | tf_op jit(solution)/shard_map/pallas_call | solution.py:697
  34.9 1.2 %copy.9 = f32[1,128]{1,0:T(1,128)} copy(f32[1,128]{1,0:T(1,128)} %shard_map.73) | data formatting | bytes 1024

commit v5 on v3

--- a/solution.py
+++ b/solution.py
@@ -256,11 +256,6 @@
     width = table.shape[1]
     f32 = jnp.float32
 
-    barrier = pltpu.get_barrier_semaphore()
-    for step in range(1, devices):
-        pl.semaphore_signal(
-            barrier, inc=1, device_id={"chan": (me + step) % devices}, device_id_type=MESH
-        )
     window = pl.ds(pl.multiple_of((me // 4) * LANES, LANES), LANES)
     loads = [
         pltpu.make_async_copy(src, dst, load_sem.at[n])
@@ -278,6 +273,12 @@
     ]
     for load in loads:
         load.start()
+
+    barrier = pltpu.get_barrier_semaphore()
+    for step in range(1, devices):
+        pl.semaphore_signal(
+            barrier, inc=1, device_id={"chan": (me + step) % devices}, device_id_type=MESH
+        )
 
     def send(src, dst, ssem, rsem, peer):
         return pltpu.make_async_remote_copy(
@@ -499,6 +500,11 @@
         ).wait_recv()
 
     gram = gram_full[...].astype(jnp.bfloat16).astype(f32)
+    tile = 16
+    first_tile = (lax.broadcasted_iota(jnp.int32, gram.shape, 0) % modes) // tile
+    second_tile = (lax.broadcasted_iota(jnp.int32, gram.shape, 1) % modes) // tile
+    gram = jnp.where(first_tile > second_tile, 2.0 * gram, gram)
+    pairs = sum(tile * (modes - start) for start in range(0, modes, tile))
     wide_lane = lax.broadcasted_iota(jnp.int32, (modes, LANES), 1)
     mode_ids = lax.broadcasted_iota(jnp.int32, (modes, depths), 0)
     sources = []
@@ -521,20 +527,23 @@
             mode_ids < counts_ref[owners[block]], modes_source_ref[owners[block]], 0.0
         )
         sources.append(source)
-        rows = slice((block // 2) * modes, (block // 2 + 1) * modes)
+        base = (block // 2) * modes
+        filled = 0
         for m in range(modes):
+            low = m // tile * tile
             lane = (block % 2) * modes + m
-            at = slice(m * modes, (m + 1) * modes)
-            terms_a[at, :] = (cosine[m : m + 1] * cosine + sine[m : m + 1] * sine).astype(
-                jnp.bfloat16
-            )
+            at = slice(filled, filled + modes - low)
+            filled += modes - low
+            terms_a[at, :] = (
+                cosine[m : m + 1] * cosine[low:] + sine[m : m + 1] * sine[low:]
+            ).astype(jnp.bfloat16)
             terms_b[at, :] = (
-                gram[rows, lane : lane + 1] * (source[m : m + 1] * source)
+                gram[base + low : base + modes, lane : lane + 1] * (source[m : m + 1] * source[low:])
             ).astype(jnp.bfloat16)
         norms.append(
             lax.dot_general(
-                terms_a[...],
-                terms_b[...],
+                terms_a[:pairs],
+                terms_b[:pairs],
                 (((0,), (0,)), ((), ())),
                 preferred_element_type=f32,
             )
@@ -612,15 +621,6 @@
     @pl.loop(1, devices)
     def _(step):
         peer = (me + step) % devices
-        send(surf_own, surf_recv.at[peer], surf_ssem.at[peer], surf_rsem.at[peer], peer).wait_recv()
-
-    total = jnp.sum(surf_recv[...], axis=0) / (columns // 2)
-    total_ref[...] = total
-    out_ref[...] = total_ref[pl.ds(me, 1), :] / jnp.max(total)
-
-    @pl.loop(1, devices)
-    def _(step):
-        peer = (me + step) % devices
         send(
             gram_part.at[pl.ds(pl.multiple_of(peer * 8, 8), 8), :],
             gram_recv.at[me],
@@ -634,7 +634,6 @@
         send(
             trace_send.at[peer], trace_recv.at[me], trace_ssem.at[peer], trace_rsem.at[me], peer
         ).wait_send()
-        send(surf_own, surf_recv.at[me], surf_ssem.at[peer], surf_rsem.at[me], peer).wait_send()
 
     @pl.loop(0, chunk_count)
     def _(chunk):
@@ -644,6 +643,15 @@
         @pl.when(chunk != far)
         def _():
             far_copy(chunk, far).wait_send()
+
+    @pl.loop(1, devices)
+    def _(step):
+        peer = (me + step) % devices
+        send(surf_own, surf_recv.at[peer], surf_ssem.at[peer], surf_rsem.at[peer], peer).wait()
+
+    total = jnp.sum(surf_recv[...], axis=0) / (columns // 2)
+    total_ref[...] = total
+    out_ref[...] = total_ref[pl.ds(me, 1), :] / jnp.max(total)
 
 
 def per_device_fused(

time: 34.9 us -> 33.8 us (0.968)
  Pallas kernels: 33.5 us -> 32.5 us
    pallas_call x1, Pallas kernels: 33.5 us -> 32.5 us  [per_device_fused(): pl.pallas_call(functools.partial(fused_kernel, devices), out_shape=jax.Sh...]
where the time goes in v5:
time: 33.8 us; the launch traced here: 33.7 us
  Pallas kernels  32.5 us (96%)
  local copies, waits for them, and re-layouts  1.19 us (4%)
    pallas_call x1, Pallas kernels, per_device_fused(): pl.pallas_call(functools.partial(fused_kernel, devices), out_shape=jax.Sh...  32.5 us
    unnamed x1, local copies, waits for them, and re-layouts  1.19 us

profile of v5, /device:TPU:0, one launch (start us, length us, event | category | flops | bytes accessed | tf_op | source)
XLA Modules:
  0.0 33.7 jit_solution(15748594441365718403)
XLA Ops:
  0.0 32.5 %shard_map.73 = f32[1,128]{1,0:T(1,128)} custom-call(s32[4,128]{1,0:T(4,128)} %bitcast.3, bf16[512,4096]{1,0:T(8,128)(2,1)} %bitcast.2, bf16[8,64,256]{2,1,0:T(8,128)(2,1)} %modes_hbm.1, s32[8]{0:T(128)} %counts_hbm.1, f32[8,64,512]{2,1,0:T(8,128)} %waves_hbm.1, f32[8,64,128]{2,1,0:T(8,128)} %source_hbm.1, s32[4]{0:T(128)} %owner_hbm.1), custom_call_target="tpu_custom_call" | custom-call | tf_op jit(solution)/shard_map/pallas_call | solution.py:673
  32.5 1.2 %copy.9 = f32[1,128]{1,0:T(1,128)} copy(f32[1,128]{1,0:T(1,128)} %shard_map.73) | data formatting | bytes 1024

commit v6 on v5

--- a/solution.py
+++ b/solution.py
@@ -484,8 +484,6 @@
         def _():
             add_side(step - 2)
 
-    add_core(last)
-    add_side(last - 1)
     trace_recv[me] = trace_send[me]
 
     @pl.loop(1, devices)
@@ -512,6 +510,9 @@
     waves_cos = []
     norms = []
     for block in range(blocks):
+        if block == 1:
+            add_core(last)
+            add_side(last - 1)
         wave = waves_ref[owners[block]]
         wave = jnp.where(wide_lane // quarter == me % 4, wave, 0.0)
         wave = wave + pltpu.roll(wave, quarter, 1)

time: 33.8 us -> 32.9 us (0.973)
  Pallas kernels: 32.5 us -> 31.5 us
    pallas_call x1, Pallas kernels: 32.5 us -> 31.5 us  [per_device_fused(): pl.pallas_call(functools.partial(fused_kernel, devices), out_shape=jax.Sh...]
where the time goes in v6:
time: 32.9 us; the launch traced here: 32.7 us
  Pallas kernels  31.5 us (96%)
  local copies, waits for them, and re-layouts  1.19 us (4%)
    pallas_call x1, Pallas kernels, per_device_fused(): pl.pallas_call(functools.partial(fused_kernel, devices), out_shape=jax.Sh...  31.5 us
    unnamed x1, local copies, waits for them, and re-layouts  1.19 us

profile of v6, /device:TPU:0, one launch (start us, length us, event | category | flops | bytes accessed | tf_op | source)
XLA Modules:
  0.0 32.7 jit_solution(2865253120774356051)
XLA Ops:
  0.0 31.5 %shard_map.73 = f32[1,128]{1,0:T(1,128)} custom-call(s32[4,128]{1,0:T(4,128)} %bitcast.3, bf16[512,4096]{1,0:T(8,128)(2,1)} %bitcast.2, bf16[8,64,256]{2,1,0:T(8,128)(2,1)} %modes_hbm.1, s32[8]{0:T(128)} %counts_hbm.1, f32[8,64,512]{2,1,0:T(8,128)} %waves_hbm.1, f32[8,64,128]{2,1,0:T(8,128)} %source_hbm.1, s32[4]{0:T(128)} %owner_hbm.1), custom_call_target="tpu_custom_call" | custom-call | tf_op jit(solution)/shard_map/pallas_call | solution.py:674
  31.5 1.2 %copy.9 = f32[1,128]{1,0:T(1,128)} copy(f32[1,128]{1,0:T(1,128)} %shard_map.73) | data formatting | bytes 1024
